TPU v7x, 256 devices: a whole 4x4x8 slice. The times are simulated.
256 devices in a mesh: group: 16 (over y, x), local: 16 (over z, core).
Axes of the slice: x: 4, y: 4, z: 8, core: 2. Of those that a mesh axis runs over, the one named last changes fastest.
Arguments:
- event_embed: bfloat16 [1024, 20, 128, 64], P(('group', 'local')), may hold values from -6 to 6
- target: bfloat16 [1024, 20, 64], P(('group', 'local')), may hold values from -6 to 6
- pooled_grad: bfloat16 [1024, 20, 64], P(('group', 'local')), may hold values from -6 to 6
- event_table: int32 [1024, 20, 128], P(('group', 'local')), may hold values from 0 to 127, as said below
- event_row: int32 [1024, 20, 128], P(('group', 'local')), may hold values from 0 to 16383
- table_slot: int32 [128], replicated, may hold values from 0 to 127, as said below
- lengths: int32 [1024, 20], P(('group', 'local')), may hold values from 64 to 128
- caps: int32 [20], replicated, may hold values from 64 to 128, as said below
- w_first: float32 [20, 256, 80], replicated, may hold values from -0.375 to 0.375
- b_first: float32 [20, 80], replicated, may hold values from -3 to 3
- w_second: float32 [20, 80, 40], replicated, may hold values from -0.625 to 0.625
- b_second: float32 [20, 40], replicated, may hold values from -3 to 3
- w_score: float32 [20, 40], replicated, may hold values from -1 to 1
Outputs:
- table_grad: float32 [128, 16384, 64], P('group', 'local')
Inputs may be any that keep to these rules, and one draw needn't show every extreme that they name: table_slot is a permutation; the tables with places g * 8 to (g + 1) * 8 - 1 belong to index g of group. `event_table`: the 10240 event slots of one device's samples, padding included, name rows held by any one device (table place // 8 as group index, row // 1024 as local index) at most 60 times, and some device exactly 60 times. `caps`: some feature's cap is 128.
All inputs are finite; a program needn't handle non-finite values.
Results may differ from a plain program's by a relative error of at most 0.0003.
Values sent between devices are 32-bit elements; how exact they have to be, the bound alone decides.
No kernel may reach another device: no remote copies, remote signals or barrier semaphores. Data moves between devices by JAX's collectives and lax.ppermute only.
A program may use at most 128 MiB of HBM per device.

v0:
```python
import math

import jax
import jax.numpy as jnp
from jax import lax
from jax.sharding import PartitionSpec as P

TAB_OWN = 8
ROWS_DEV = 1024


def silu_slope(value):
    sig = jax.nn.sigmoid(value)
    return sig * (1.0 + value * (1.0 - sig))


def event_grads(
    embeds, target, pooled_grad, lengths, caps, w_first, b_first, w_second, b_second, w_score
):
    hp = lax.Precision.HIGHEST
    width = embeds.shape[-1]
    vecs = embeds.astype(jnp.float32)
    query = jnp.broadcast_to(target.astype(jnp.float32)[:, :, None, :], vecs.shape)
    joined = jnp.concatenate([vecs, query, vecs * query, vecs - query], axis=-1)
    pre_first = (
        jnp.einsum("nftk,fkh->nfth", joined, w_first, precision=hp) + b_first[None, :, None, :]
    )
    hidden_one = jax.nn.silu(pre_first)
    pre_second = (
        jnp.einsum("nfth,fhj->nftj", hidden_one, w_second, precision=hp)
        + b_second[None, :, None, :]
    )
    hidden_two = jax.nn.silu(pre_second)
    score = jnp.einsum("nftj,fj->nft", hidden_two, w_score, precision=hp)
    limit = jnp.minimum(lengths, caps[None, :])
    slots = jnp.arange(vecs.shape[2], dtype=jnp.int32)
    kept_mask = (slots[None, None, :] < limit[:, :, None]).astype(jnp.float32)
    upstream = pooled_grad.astype(jnp.float32)[:, :, None, :]
    dscore = jnp.sum(upstream * vecs, axis=-1)
    d_second = dscore[..., None] * w_score[None, :, None, :] * silu_slope(pre_second)
    d_hidden = jnp.einsum("nftj,fhj->nfth", d_second, w_second, precision=hp)
    d_first = d_hidden * silu_slope(pre_first)
    d_joined = jnp.einsum("nfth,fkh->nftk", d_first, w_first, precision=hp)
    total = (
        score[..., None] * upstream
        + d_joined[..., :width]
        + d_joined[..., 2 * width : 3 * width] * query
        + d_joined[..., 3 * width :]
    )
    return total * kept_mask[..., None]


def per_device(
    event_embed,
    target,
    pooled_grad,
    event_table,
    event_row,
    table_slot,
    lengths,
    caps,
    w_first,
    b_first,
    w_second,
    b_second,
    w_score,
):
    highest = lax.Precision.HIGHEST
    width = event_embed.shape[-1]
    groups = lax.axis_size("group")
    locals_count = lax.axis_size("local")
    dev_count = groups * locals_count
    grads = event_grads(
        event_embed,
        target,
        pooled_grad,
        lengths,
        caps,
        w_first,
        b_first,
        w_second,
        b_second,
        w_score,
    )
    slot_count = grads.shape[0] * grads.shape[1] * grads.shape[2]
    capacity = 3 * (slot_count // dev_count) // 2
    buffer_len = dev_count * capacity
    flat_grads = grads.reshape(slot_count, width)
    table_ids = event_table.reshape(slot_count)
    table_count = table_slot.shape[0]
    table_hits = table_ids[:, None] == jnp.arange(table_count, dtype=jnp.int32)[None, :]
    places = jnp.sum(jnp.where(table_hits, table_slot[None, :], 0), axis=1)
    rows = event_row.reshape(slot_count)
    target_dev = places // TAB_OWN * locals_count + rows // ROWS_DEV
    row_place = (places % TAB_OWN * ROWS_DEV + rows % ROWS_DEV).astype(jnp.float32)
    slot_block = math.gcd(slot_count, 512)
    block_count = slot_count // slot_block
    dev_hits = (target_dev[:, None] == jnp.arange(dev_count, dtype=jnp.int32)[None, :]).astype(
        jnp.bfloat16
    )
    dev_hits = dev_hits.reshape(block_count, slot_block, dev_count)
    inner_iota = jnp.arange(slot_block, dtype=jnp.int32)
    earlier = (inner_iota[:, None] > inner_iota[None, :]).astype(jnp.bfloat16)
    within = jnp.einsum("ij,bjd->bid", earlier, dev_hits, preferred_element_type=jnp.float32)
    block_totals = jnp.sum(dev_hits.astype(jnp.float32), axis=1)
    outer_iota = jnp.arange(block_count, dtype=jnp.int32)
    block_earlier = (outer_iota[:, None] > outer_iota[None, :]).astype(jnp.float32)
    offsets = jnp.dot(block_earlier, block_totals, precision=highest)
    position = jnp.sum(dev_hits.astype(jnp.float32) * (within + offsets[:, None, :]), axis=2)
    position = position.reshape(slot_count).astype(jnp.int32)
    buffer_index = target_dev * capacity + position
    packed_grads = jnp.zeros((buffer_len, width), jnp.float32).at[buffer_index].set(flat_grads)
    packed_places = jnp.zeros((buffer_len,), jnp.float32).at[buffer_index].set(row_place)
    outgoing = packed_grads.reshape(groups, locals_count, capacity, width)
    outgoing_places = packed_places.reshape(groups, locals_count, capacity)
    halfway = (
        lax.all_to_all(outgoing, "group", split_axis=0, concat_axis=0, tiled=True),
        lax.all_to_all(outgoing_places, "group", split_axis=0, concat_axis=0, tiled=True),
    )
    arrived, arrived_places = (
        lax.all_to_all(halfway[0], "local", split_axis=1, concat_axis=1, tiled=True),
        lax.all_to_all(halfway[1], "local", split_axis=1, concat_axis=1, tiled=True),
    )
    landing = arrived_places.reshape(-1).astype(jnp.int32)
    flat_arrived = arrived.reshape(-1, width)
    total_rows = TAB_OWN * ROWS_DEV
    summed = jnp.zeros((total_rows, width), jnp.float32).at[landing].add(flat_arrived)
    return summed.reshape(TAB_OWN, ROWS_DEV, width)


def solution(mesh):
    in_specs = (
        P(("group", "local"), None, None, None),
        P(("group", "local"), None, None),
        P(("group", "local"), None, None),
        P(("group", "local"), None, None),
        P(("group", "local"), None, None),
        P(),
        P(("group", "local"), None),
        P(),
        P(),
        P(),
        P(),
        P(),
        P(),
    )
    out_specs = P("group", "local", None)
    return jax.shard_map(
        per_device, mesh=mesh, in_specs=in_specs, out_specs=out_specs, check_vma=False
    )
```

profile of v0, /device:TPU:1, one launch (start us, length us, event | category | flops | bytes accessed | tf_op | source)
XLA Modules:
  0.0 526.9 jit_solution(8476723606814686683)
XLA Ops:
  1.8 7.0 %select_reduce_fusion = s32[10240]{0:T(1024)S(1)} fusion(s32[128]{0:T(128)} %param.18, s32[10240]{0:T(1024)S(1)} %eq.33), kind=kLoop, calls=%fused_computation.24 | loop fusion | flops 3921920 | bytes 82432 | tf_op jit(solution)/shard_map/reduce_sum | solution.py:92
  10.1 4.7 fusion
  15.4 38.0 %scatter_custom_fusion = f32[15360]{0:T(1024)S(1)} fusion(s32[10240]{0:T(1024)S(1)} %bitcast.112, f32[10240]{0:T(1024)S(1)} %fusion.70, f32[]{:T(128)} %constant.57.clone.1), kind=kCustom, calls=%fused_computation.117 | custom fusion | bytes 61444 | tf_op jit(solution)/shard_map/scatter | solution.py:113
  54.5 7.6 %all-to-all-start = ((f32[16,1,960]{2,1,0:T(1,128)}), f32[16,1,960]{2,1,0:T(1,128)S(1)}, u32[]{:S(2)}, u32[]{:S(2)}) async-start(f32[16,1,960]{2,1,0:T(1,128)} %reshape.285), calls=%async_computation | async-start | bytes 131072 | tf_op jit(solution)/shard_map/all_to_all | solution.py:118
  62.1 2.9 copy.74
  65.0 4.9 convert_element_type.62
  69.9 1.5 convert_multiply_fusion.1
  71.8 15.5 %fusion.1 = f32[20,4,128,80]{2,3,1,0:T(8,128)S(1)} fusion(f32[4,20,128,64]{3,2,0,1:T(8,128)S(1)} %get-tuple-element.6, f32[4,20,128,64]{3,2,0,1:T(8,128)S(1)} %get-tuple-element.5, f32[4,20,128,64]{3,2,0,1:T(8,128)S(1)} %broadcast_in_dim.21, f32[4,20,128,64]{3,2,0,1:T(8,128)} %convert_element_type.62, f32[20,256,80]{1,2,0:T(8,128)S(1)} %copy-done), kind=kOutput, calls=%fused_computation.6 | convolution fusion | flops 2524446720 | bytes 15400960 | tf_op jit(solution)/shard_map/nftk,fkh->nfth/dot_general | solution.py:26
  87.4 2.6 fusion.19
  90.0 3.6 fusion.39
  93.7 12.3 %convolution_bitcast_fusion = f32[4,20,128,256]{3,2,0,1:T(8,128)} fusion(f32[20,4,128,80]{2,3,1,0:T(8,128)S(1)} %fusion.39, f32[20,4,128,80]{2,3,1,0:T(8,128)S(1)} %fusion.1, f32[20,256,80]{1,2,0:T(8,128)S(1)} %copy-done, f32[20,80]{1,0:T(8,128)S(1)} %copy-done.6), kind=kOutput, calls=%fused_computation.30 | convolution fusion | flops 2523955200 | bytes 18684160 | tf_op jit(solution)/shard_map/nfth,fkh->nftk/dot_general | solution.py:43
  107.6 9.6 %fusion.11 = f32[4,20,128,64]{3,2,0,1:T(8,128)S(1)} fusion(f32[4,20,128,256]{3,2,0,1:T(8,128)} %convolution_bitcast_fusion, f32[4,20,128]{2,0,1:T(4,128)S(1)} %fusion.72, f32[4,20,64]{2,0,1:T(4,128)S(1)} %convert_element_type.64, f32[4,20,128]{2,0,1:T(4,128)S(1)} %bitcast.111, f32[4,20,64]{2,0,1:T(4,128)S(1)} %convert_element_type.63), kind=kLoop, calls=%fused_computation.18 | loop fusion | flops 3932160 | bytes 10608640 | tf_op jit(solution)/shard_map/mul | solution.py:50
  117.2 2.9 copy.89
  120.1 29.4 %scatter_custom_fusion.1 = f32[15360,64]{1,0:T(8,128)} fusion(s32[10240]{0:T(1024)S(1)} %bitcast.113, f32[10240,64]{1,0:T(8,128)} %bitcast.106, f32[]{:T(128)} %constant.57.clone.1), kind=kCustom, calls=%fused_computation.28 | custom fusion | bytes 3932672 | tf_op jit(solution)/shard_map/scatter | solution.py:112
  149.5 9.0 %reshape.277 = f32[16,16,60,64]{3,2,1,0:T(8,128)} reshape(f32[15360,64]{1,0:T(8,128)} %scatter_custom_fusion.1) | data formatting | bytes 7864320 | tf_op jit(solution)/shard_map/reshape | solution.py:114
  158.5 12.6 %copy.103 = f32[16,16,60,64]{3,1,2,0:T(8,128)} copy(f32[16,16,60,64]{3,2,1,0:T(8,128)} %reshape.277) | data formatting | bytes 7864320 | tf_op jit(solution)/shard_map/reshape | solution.py:114
  171.1 12.9 %reshape.289 = f32[16,1,61440]{2,1,0:T(1,128)} reshape(f32[16,60,16,64]{3,2,1,0:T(8,128)} %bitcast.101) | data formatting | bytes 7864320
  184.0 6.9 %all-to-all-start.2 = ((f32[16,1,61440]{2,1,0:T(1,128)}), f32[16,1,61440]{2,1,0:T(1,128)}, u32[]{:S(2)}, u32[]{:S(2)}) async-start(f32[16,1,61440]{2,1,0:T(1,128)} %reshape.289), calls=%async_computation.2 | async-start | bytes 7864320 | tf_op jit(solution)/shard_map/all_to_all | solution.py:117
  193.4 54.5 %all-to-all-done.2 = f32[16,1,61440]{2,1,0:T(1,128)} async-done(((f32[16,1,61440]{2,1,0:T(1,128)}), f32[16,1,61440]{2,1,0:T(1,128)}, u32[]{:S(2)}, u32[]{:S(2)}) %all-to-all-start.2) | async-done | bytes 3932192 | tf_op jit(solution)/shard_map/all_to_all | solution.py:117
  247.8 10.9 %all-to-all-start.1 = ((f32[16,1,960]{2,1,0:T(1,128)}), f32[16,1,960]{2,1,0:T(1,128)S(1)}, u32[]{:S(2)}, u32[]{:S(2)}) async-start(f32[16,1,960]{2,1,0:T(1,128)} %reshape.287), calls=%async_computation.1 | async-start | bytes 131072 | tf_op jit(solution)/shard_map/all_to_all | solution.py:122
  258.7 13.1 %reduce.2 = f32[16,61440]{1,0:T(8,128)} reduce(f32[16,1,61440]{2,1,0:T(1,128)} %all-to-all-done.2, f32[]{:T(128)} %broadcast.239), dimensions={1}, to_apply=%all_to_all.14.reduce_sub_computation | reduce | bytes 7864324 | tf_op jit(solution)/shard_map/all_to_all | solution.py:117
  271.8 6.6 %reshape.290 = f32[16,60,16,64]{3,2,1,0:T(8,128)} reshape(f32[16,61440]{1,0:T(8,128)} %reduce.2) | data formatting | bytes 7864320
  278.4 10.9 %copy.104 = f32[16,16,60,64]{3,0,2,1:T(8,128)} copy(f32[16,16,60,64]{3,1,2,0:T(8,128)} %bitcast.102) | data formatting | bytes 7864320 | tf_op jit(solution)/shard_map/all_to_all | solution.py:117
  289.4 12.9 %reshape.291 = f32[16,1,61440]{2,1,0:T(1,128)} reshape(f32[16,60,16,64]{3,2,1,0:T(8,128)} %bitcast.103) | data formatting | bytes 7864320
  302.3 7.6 %all-to-all-start.3 = ((f32[16,1,61440]{2,1,0:T(1,128)}), f32[16,1,61440]{2,1,0:T(1,128)}, u32[]{:S(2)}, u32[]{:S(2)}) async-start(f32[16,1,61440]{2,1,0:T(1,128)} %reshape.291), calls=%async_computation.3 | async-start | bytes 7864320 | tf_op jit(solution)/shard_map/all_to_all | solution.py:121
  311.2 86.6 %all-to-all-done.3 = f32[16,1,61440]{2,1,0:T(1,128)} async-done(((f32[16,1,61440]{2,1,0:T(1,128)}), f32[16,1,61440]{2,1,0:T(1,128)}, u32[]{:S(2)}, u32[]{:S(2)}) %all-to-all-start.3) | async-done | bytes 3932192 | tf_op jit(solution)/shard_map/all_to_all | solution.py:121
  397.7 13.1 %reduce.3 = f32[16,61440]{1,0:T(8,128)} reduce(f32[16,1,61440]{2,1,0:T(1,128)} %all-to-all-done.3, f32[]{:T(128)} %broadcast.239), dimensions={1}, to_apply=%all_to_all.15.reduce_sub_computation | reduce | bytes 7864324 | tf_op jit(solution)/shard_map/all_to_all | solution.py:121
  410.8 6.6 %reshape.292 = f32[16,60,16,64]{3,2,1,0:T(8,128)} reshape(f32[16,61440]{1,0:T(8,128)} %reduce.3) | data formatting | bytes 7864320
  417.4 9.0 %copy.92 = f32[16,16,60,64]{3,2,1,0:T(8,128)} copy(f32[16,16,60,64]{3,0,2,1:T(8,128)} %bitcast.104) | data formatting | bytes 7864320 | tf_op jit(solution)/shard_map/reshape | solution.py:125
  426.4 9.0 %reshape.278 = f32[15360,64]{1,0:T(8,128)} reshape(f32[16,16,60,64]{3,2,1,0:T(8,128)} %copy.92) | data formatting | bytes 7864320 | tf_op jit(solution)/shard_map/reshape | solution.py:125
  435.3 87.3 %scatter_custom_fusion.2 = f32[8192,64]{1,0:T(8,128)} fusion(s32[15360]{0:T(1024)S(1)} %bitcast.110, f32[15360,64]{1,0:T(8,128)} %reshape.278, f32[]{:T(128)} %constant.57.clone.1), kind=kCustom, calls=%fused_computation.44 | custom fusion | flops 983040 | bytes 2097664 | tf_op jit(solution)/shard_map/scatter-add | solution.py:127
  522.7 3.8 copy.84
  (60 shorter events, 10.3 us)
Async XLA Ops:
  0.0 71.8 %copy-start = (f32[20,256,80]{1,2,0:T(8,128)S(1)}, f32[20,256,80]{1,2,0:T(8,128)}, u32[]{:S(2)}) copy-start(f32[20,256,80]{1,2,0:T(8,128)} %param.21) | copy-start | bytes 4915204
  10.1 51.9 %copy-start.3 = (bf16[4,20,128,64]{2,3,1,0:T(8,128)(2,1)S(1)}, bf16[4,20,128,64]{2,3,1,0:T(8,128)(2,1)}, u32[]{:S(2)}) copy-start(bf16[4,20,128,64]{2,3,1,0:T(8,128)(2,1)} %param.13) | copy-start | bytes 3932164
  14.8 50.1 %copy-start.4 = (bf16[4,20,64]{2,0,1:T(4,128)(2,1)S(1)}, bf16[4,20,64]{2,0,1:T(4,128)(2,1)}, u32[]{:S(2)}) copy-start(bf16[4,20,64]{2,0,1:T(4,128)(2,1)} %param.14) | copy-start | bytes 30724
  14.8 50.2 %copy-start.5 = (bf16[4,20,64]{2,0,1:T(4,128)(2,1)S(1)}, bf16[4,20,64]{2,0,1:T(4,128)(2,1)}, u32[]{:S(2)}) copy-start(bf16[4,20,64]{2,0,1:T(4,128)(2,1)} %param.15) | copy-start | bytes 30724
  54.5 129.6 %all-to-all-start = ((f32[16,1,960]{2,1,0:T(1,128)}), f32[16,1,960]{2,1,0:T(1,128)S(1)}, u32[]{:S(2)}, u32[]{:S(2)}) async-start(f32[16,1,960]{2,1,0:T(1,128)} %reshape.285), calls=%async_computation | async-start | bytes 131072 | tf_op jit(solution)/shard_map/all_to_all | solution.py:118
  65.0 4.9 copy-start.2
  71.8 15.6 %copy-start.6 = (f32[20,80]{1,0:T(8,128)S(1)}, f32[20,80]{1,0:T(8,128)}, u32[]{:S(2)}) copy-start(f32[20,80]{1,0:T(8,128)} %param.22) | copy-start | bytes 19204
  71.8 15.6 %copy-start.9 = (f32[20,80,40]{1,2,0:T(8,128)S(1)}, f32[20,80,40]{1,2,0:T(8,128)}, u32[]{:S(2)}) copy-start(f32[20,80,40]{1,2,0:T(8,128)} %param.23) | copy-start | bytes 768004
  87.4 2.7 copy-start.10
  87.4 2.7 copy-start.11
  105.9 1.4 copy-start.7
  105.9 1.4 copy-start.8
  184.0 63.8 %all-to-all-start.2 = ((f32[16,1,61440]{2,1,0:T(1,128)}), f32[16,1,61440]{2,1,0:T(1,128)}, u32[]{:S(2)}, u32[]{:S(2)}) async-start(f32[16,1,61440]{2,1,0:T(1,128)} %reshape.289), calls=%async_computation.2 | async-start | bytes 7864320 | tf_op jit(solution)/shard_map/all_to_all | solution.py:117
  247.8 54.5 %all-to-all-start.1 = ((f32[16,1,960]{2,1,0:T(1,128)}), f32[16,1,960]{2,1,0:T(1,128)S(1)}, u32[]{:S(2)}, u32[]{:S(2)}) async-start(f32[16,1,960]{2,1,0:T(1,128)} %reshape.287), calls=%async_computation.1 | async-start | bytes 131072 | tf_op jit(solution)/shard_map/all_to_all | solution.py:122
  302.3 95.4 %all-to-all-start.3 = ((f32[16,1,61440]{2,1,0:T(1,128)}), f32[16,1,61440]{2,1,0:T(1,128)}, u32[]{:S(2)}, u32[]{:S(2)}) async-start(f32[16,1,61440]{2,1,0:T(1,128)} %reshape.291), calls=%async_computation.3 | async-start | bytes 7864320 | tf_op jit(solution)/shard_map/all_to_all | solution.py:121
  435.3 91.1 %copy-start.1 = (f32[20,256,80]{1,2,0:T(8,128)S(1)}, f32[20,256,80]{1,2,0:T(8,128)}, u32[]{:S(2)}) copy-start(f32[20,256,80]{1,2,0:T(8,128)} %param.21) | copy-start | bytes 4915204
where the time goes:
time: 534 us; the launch traced here: 527 us
  local copies, waits for them, and re-layouts  172 us (32%)
  waiting for transfers between devices  141 us (26%)
  other arithmetic  140 us (26%)
  matrix products  40.3 us (8%)
  starting transfers between devices  33 us (6%)
    scatter-add x1, other arithmetic, per_device(): jnp.zeros((total_rows, width), jnp.float32).at[landing].add(flat_arrived)  87.3 us
    all_to_all x1, waiting for transfers between devices, per_device(): lax.all_to_all(halfway[0], 'local', split_axis=1, concat_axis=1, tiled=True)  86.6 us
    all_to_all x1, waiting for transfers between devices, per_device(): lax.all_to_all(outgoing, 'group', split_axis=0, concat_axis=0, tiled=True)  54.5 us
    unnamed x36, local copies, waits for them, and re-layouts  45.7 us
    scatter x1, local copies, waits for them, and re-layouts, per_device(): jnp.zeros((buffer_len,), jnp.float32).at[buffer_index].set(row_place)  38 us
    scatter x1, local copies, waits for them, and re-layouts, per_device(): jnp.zeros((buffer_len, width), jnp.float32).at[buffer_index].set(flat_grads)  29.4 us
    reshape x2, local copies, waits for them, and re-layouts, per_device(): outgoing = packed_grads.reshape(groups, locals_count, capacity, width)  21.6 us
    reshape x2, local copies, waits for them, and re-layouts, per_device(): flat_arrived = arrived.reshape(-1, width)  18 us
  transfers between devices with their start and end apart: 4, of which 2 were waited for; matrix products, arithmetic and copies ran while one was open for 32% of the time, Pallas kernels for 0%

commit v1 on v0

v1 whole, which is shorter than its diff:
```python
import functools

import jax
import jax.numpy as jnp
from jax import lax
from jax.experimental import pallas as pl
from jax.experimental.pallas import tpu as pltpu
from jax.sharding import PartitionSpec as P

D = 64
F = 20
H1 = 80
H2 = 40
LMAX = 128
B_DEV = 4
TAB_OWN = 8
ROWS_DEV = 1024
GROUPS = 16
LOCALS = 16
DEVS = GROUPS * LOCALS
PAIRS = B_DEV * F
ROWS_OWN = TAB_OWN * ROWS_DEV
BUCKET = 64
HALF = 32
DUMMY = DEVS * BUCKET
BF = jnp.bfloat16
F32 = jnp.float32
VMEM_BYTES = 56 * 1024 * 1024


def dot(left, right, contract=((1,), (0,))):
    return lax.dot_general(
        left, right, (contract, ((), ())), preferred_element_type=F32
    )


def index_kernel(len_ref, cap_ref, table_ref, row_ref, places_ref, slots_ref, out_ref, dev_ref, own_ref, carry_ref):
    table = table_ref[...]
    place = jnp.take_along_axis(
        jnp.broadcast_to(places_ref[...], table.shape), table, axis=1, mode="promise_in_bounds"
    )
    row = row_ref[...]
    dev_ref[...] = (place >> 3) * LOCALS + (row >> 10)
    own_ref[...] = (place & 7) * ROWS_DEV + (row & 1023)
    carry_ref[...] = jnp.zeros_like(carry_ref)
    out_ref[...] = jnp.zeros_like(out_ref)
    lane = lax.broadcasted_iota(jnp.int32, (1, LMAX), 1)
    dev_iota = lax.broadcasted_iota(jnp.int32, (DEVS, LMAX), 0)
    tri_row = lax.broadcasted_iota(jnp.int32, (LMAX, 2 * LMAX), 0)
    tri_col = lax.broadcasted_iota(jnp.int32, (LMAX, 2 * LMAX), 1)
    earlier = ((tri_row < tri_col)).astype(F32).astype(BF)
    pos_iota = lax.broadcasted_iota(jnp.int32, (2 * BUCKET, LMAX), 0)

    def feature(f, _):
        for n in range(B_DEV):
            p = f * B_DEV + n
            limit = jnp.minimum(len_ref[n, f], cap_ref[f])
            kept = lane < limit
            dev = dev_ref[pl.ds(p, 1), :]
            own = own_ref[pl.ds(p, 1), :]
            hits = dev_iota == jnp.where(kept, dev, -1)
            hot = hits.astype(F32)
            hot_bf = hot.astype(BF)
            counts = dot(hot_bf, earlier)
            before = counts[:, :LMAX] + carry_ref[...]
            carry_ref[...] += counts[:, LMAX:]
            pos = jnp.sum(hot * before, axis=0, keepdims=True).astype(jnp.int32)
            slot = dev * BUCKET + (pos & 1) * HALF + (pos >> 1)
            slots_ref[pl.ds(p, 1), :] = jnp.where(kept, slot, DUMMY)
            value = jnp.where(
                pos_iota < BUCKET, (own >> 7) + 1, own & 127
            )
            spread = jnp.where((pos_iota & (BUCKET - 1)) == pos, value, 0)
            out_ref[...] += dot(hot_bf, spread.astype(F32).astype(BF), ((1,), (1,)))
        return 0

    lax.fori_loop(0, F, feature, 0)
    parts = out_ref[...]
    high = pltpu.roll(parts, BUCKET, 1)
    out_ref[...] = jnp.where(high > 0.0, high * 128.0 + parts - 128.0, float(ROWS_OWN))


def to_column(row, size):
    rows = lax.broadcasted_iota(jnp.int32, (size, row.shape[1]), 0)
    cols = lax.broadcasted_iota(jnp.int32, (size, row.shape[1]), 1)
    return jnp.where(rows == cols, row, 0.0)


def split(value):
    high = value.astype(BF)
    low = (value - high.astype(F32)).astype(BF)
    return high, low


def grad_kernel(
    slots_ref,
    event_ref,
    query_ref,
    up_ref,
    w1_ref,
    b1_ref,
    w2_ref,
    b2_ref,
    ws_ref,
    place_ref,
    out_ref,
    bucket_ref,
    grad_ref,
):
    f = pl.program_id(0)
    w1 = w1_ref[0]
    wa, wb, wc, wd = (w1[:, i * D : (i + 1) * D] for i in range(4))
    wad = wa + wd
    wbd = wb - wd
    wad = jnp.concatenate([wad, wad], axis=1)
    wcc = jnp.concatenate([wc, wc], axis=1)
    zeros = jnp.zeros((H1, D), F32)
    wbd = jnp.concatenate([wbd, zeros], axis=1)
    b1_diag = to_column(
        jnp.concatenate([b1_ref[pl.ds(f, 1), :], jnp.zeros((1, 128 - H1), F32)], axis=1), H1
    )
    b2 = jnp.sum(to_column(b2_ref[pl.ds(f, 1), :], H2), axis=1, keepdims=True)
    ws = jnp.sum(to_column(ws_ref[pl.ds(f, 1), :], H2), axis=1, keepdims=True)
    w2t = w2_ref[0]
    w2t_hi, w2t_lo = split(w2t)
    w2_hi, w2_lo = split(w2t.T)
    w2t_all = jnp.concatenate([w2t_hi, w2t_lo, w2t_hi], axis=1)
    w2_all = jnp.concatenate([w2_hi, w2_lo, w2_hi], axis=1)
    left_half = lax.broadcasted_iota(jnp.int32, (H1, 128), 1) < D
    first_row = lax.broadcasted_iota(jnp.int32, (16, 128), 0) == 0
    row_at = lax.broadcasted_iota(jnp.int32, (16, 128), 0)
    lane_at = lax.broadcasted_iota(jnp.int32, (16, 128), 1)
    for n in range(B_DEV):
        events = event_ref[n, 0]
        query = query_ref[0, n : n + 1, :].astype(F32)
        up = up_ref[0, n : n + 1, :].astype(F32)
        query = jnp.concatenate([query, query], axis=1)
        up = jnp.concatenate([up, up], axis=1)
        folded = wad + wcc * query
        fold_hi = folded.astype(BF)
        fold_rest = folded - fold_hi.astype(F32)
        fold_lo = fold_rest.astype(BF)
        offset = jnp.sum(wbd * query + b1_diag, axis=1, keepdims=True)
        both = jnp.where(left_half, fold_hi.astype(F32), fold_rest).astype(BF)
        up_row = jnp.where((row_at == 0) & (lane_at < D), up, 0.0).astype(BF)
        first = dot(
            jnp.concatenate([both, up_row], axis=0), jnp.concatenate([events, events], axis=0)
        )
        pre1 = first[:H1] + offset
        dscore = first[H1 : H1 + 1]
        sig1 = 0.5 + 0.5 * jnp.tanh(0.5 * pre1)
        h1 = pre1 * sig1
        slope1 = sig1 + h1 * (1.0 - sig1)
        h1_hi, h1_lo = split(h1)
        pre2 = dot(w2t_all, jnp.concatenate([h1_hi, h1_hi, h1_lo], axis=0)) + b2
        sig2 = 0.5 + 0.5 * jnp.tanh(0.5 * pre2)
        h2 = pre2 * sig2
        slope2 = sig2 + h2 * (1.0 - sig2)
        score = jnp.sum(h2 * ws, axis=0, keepdims=True)
        d2 = (dscore * ws) * slope2
        d2_hi, d2_lo = split(d2)
        d1 = dot(w2_all, jnp.concatenate([d2_hi, d2_hi, d2_lo], axis=0)) * slope1
        d1_hi, d1_lo = split(d1)
        score_hi = score.astype(BF).astype(F32)
        score_rows = jnp.where(
            row_at == 0, score_hi, jnp.where(row_at == 1, score - score_hi, 0.0)
        ).astype(BF)
        up_rows = jnp.where(row_at < 2, up, 0.0).astype(BF)
        grad_ref[n * LMAX : (n + 1) * LMAX, :] = dot(
            jnp.concatenate([d1_hi, d1_lo, d1_hi, score_rows], axis=0),
            jnp.concatenate([fold_hi, fold_hi, fold_lo, up_rows], axis=0),
            ((0,), (0,)),
        )
    base = f * (B_DEV * LMAX)

    for t in range(B_DEV * LMAX):
        slot = slots_ref[base + t]
        bucket_ref[pl.ds(slot, 1), :] = grad_ref[t : t + 1, :]

    @pl.when(f == F - 1)
    def _():
        lanes = lax.broadcasted_iota(jnp.int32, (HALF, 128), 1) < D

        def pack(dev, _):
            at = pl.multiple_of(dev * BUCKET, BUCKET)
            bucket_ref[pl.ds(at + BUCKET - 1, 1), :] = place_ref[pl.ds(dev, 1), :]
            left = bucket_ref[pl.ds(at, HALF), :]
            right = bucket_ref[pl.ds(pl.multiple_of(at + HALF, HALF), HALF), :]
            out_ref[dev] = jnp.where(lanes, left, right)
            return 0

        lax.fori_loop(0, DEVS, pack, 0, unroll=4)


def landing_kernel(tail_ref, out_ref):
    values = tail_ref[:, 7, :].astype(jnp.int32)
    lane = lax.broadcasted_iota(jnp.int32, values.shape, 1)
    filled = (lane >= D) & (values < ROWS_OWN)
    count = jnp.sum(filled.astype(jnp.int32), axis=1, keepdims=True)
    clash = jnp.zeros(values.shape, jnp.int32)
    for shift in range(2, 16, 2):
        moved = pltpu.roll(values, shift, 1)
        same = filled & (moved == values) & ((lane & 15) >= shift)
        clash = clash | same.astype(jnp.int32)
    clashes = jnp.sum(clash, axis=1, keepdims=True)
    batches = (count + 15) >> 4
    result = jnp.where(lane == 0, batches, values)
    out_ref[...] = jnp.where(lane == 1, clashes, result)


def add_kernel(land_ref, in_ref, out_ref, left_ref, right_ref):
    def clear(i, _):
        at = pl.multiple_of(i * 64, 64)
        left_ref[pl.ds(at, 64), :] = jnp.zeros((64, 128), F32)
        right_ref[pl.ds(at, 64), :] = jnp.zeros((64, 128), F32)
        return 0

    lax.fori_loop(0, ROWS_OWN // 64, clear, 0)

    def source(s, _):
        base = s * 128
        batches = land_ref[base]
        clashes = land_ref[base + 1]

        def batch(b, _):
            at = base + D + b * 16
            row = s * HALF + b * 8
            spots_l = [land_ref[at + 2 * j] for j in range(8)]
            spots_r = [land_ref[at + 2 * j + 1] for j in range(8)]
            news = [in_ref[pl.ds(row + j, 1), :] for j in range(8)]
            left = [left_ref[pl.ds(spots_l[j], 1), :] + news[j] for j in range(8)]
            right = [right_ref[pl.ds(spots_r[j], 1), :] + news[j] for j in range(8)]
            for j in range(8):
                left_ref[pl.ds(spots_l[j], 1), :] = left[j]
            for j in range(8):
                right_ref[pl.ds(spots_r[j], 1), :] = right[j]
            return 0

        def single(j, _):
            at = base + D + 2 * j
            spot_l = land_ref[at]
            spot_r = land_ref[at + 1]
            new = in_ref[pl.ds(s * HALF + j, 1), :]
            left_ref[pl.ds(spot_l, 1), :] += new
            right_ref[pl.ds(spot_r, 1), :] += new
            return 0

        @pl.when(clashes == 0)
        def _():
            lax.fori_loop(0, batches, batch, 0)

        @pl.when(clashes != 0)
        def _():
            lax.fori_loop(0, batches * 8, single, 0)

        return 0

    lax.fori_loop(0, DEVS, source, 0)
    lanes = lax.broadcasted_iota(jnp.int32, (128, 128), 1) < D

    for table in range(TAB_OWN):
        for block in range(ROWS_DEV // 128):
            at = table * ROWS_DEV + block * 128
            joined = jnp.where(lanes, left_ref[at : at + 128, :], right_ref[at : at + 128, :])
            turned = joined.T
            out_ref[table, :, block * 128 : (block + 1) * 128] = turned[:D] + turned[D:]


def params(semantics=None):
    return pltpu.CompilerParams(vmem_limit_bytes=VMEM_BYTES, dimension_semantics=semantics)


def find_slots(lengths, caps, table, row, places):
    smem = pl.BlockSpec(memory_space=pltpu.SMEM)
    vmem = pl.BlockSpec(memory_space=pltpu.VMEM)
    return pl.pallas_call(
        index_kernel,
        in_specs=[smem, smem, vmem, vmem, vmem],
        out_specs=[vmem, vmem],
        out_shape=[
            jax.ShapeDtypeStruct((PAIRS, LMAX), jnp.int32),
            jax.ShapeDtypeStruct((DEVS, LMAX), F32),
        ],
        scratch_shapes=[
            pltpu.VMEM((PAIRS, LMAX), jnp.int32),
            pltpu.VMEM((PAIRS, LMAX), jnp.int32),
            pltpu.VMEM((DEVS, LMAX), F32),
        ],
        compiler_params=params(),
    )(lengths, caps, table, row, places)


def pack_grads(slots, events, query, up, w1, b1, w2, b2, ws, place):
    whole = lambda shape: pl.BlockSpec(shape, lambda f, s: (0,) * len(shape))
    return pl.pallas_call(
        grad_kernel,
        grid_spec=pltpu.PrefetchScalarGridSpec(
            num_scalar_prefetch=1,
            grid=(F,),
            in_specs=[
                pl.BlockSpec((B_DEV, 1, D, LMAX), lambda f, s: (0, f, 0, 0)),
                pl.BlockSpec((1, B_DEV, D), lambda f, s: (f, 0, 0)),
                pl.BlockSpec((1, B_DEV, D), lambda f, s: (f, 0, 0)),
                pl.BlockSpec((1, H1, 4 * D), lambda f, s: (f, 0, 0)),
                whole((F, H1)),
                pl.BlockSpec((1, H2, H1), lambda f, s: (f, 0, 0)),
                whole((F, H2)),
                whole((F, H2)),
                whole((DEVS, LMAX)),
            ],
            out_specs=pl.BlockSpec((DEVS, HALF, 128), lambda f, s: (0, 0, 0)),
            scratch_shapes=[
                pltpu.VMEM((DUMMY + 8, 128), F32),
                pltpu.VMEM((B_DEV * LMAX, 128), F32),
            ],
        ),
        out_shape=jax.ShapeDtypeStruct((DEVS, HALF, 128), F32),
        compiler_params=params(("arbitrary",)),
    )(slots, events, query, up, w1, b1, w2, b2, ws, place)


def find_landing(arrived):
    return pl.pallas_call(
        landing_kernel,
        grid=(1,),
        in_specs=[pl.BlockSpec((DEVS, 8, 128), lambda i: (0, 3, 0))],
        out_specs=pl.BlockSpec((DEVS, 128), lambda i: (0, 0)),
        out_shape=jax.ShapeDtypeStruct((DEVS, 128), jnp.int32),
        compiler_params=params(("arbitrary",)),
    )(arrived)


def add_rows(landing, arrived):
    return pl.pallas_call(
        add_kernel,
        grid_spec=pltpu.PrefetchScalarGridSpec(
            num_scalar_prefetch=1,
            grid=(1,),
            in_specs=[pl.BlockSpec((DEVS * HALF, 128), lambda i, s: (0, 0))],
            out_specs=pl.BlockSpec((TAB_OWN, D, ROWS_DEV), lambda i, s: (0, 0, 0)),
            scratch_shapes=[
                pltpu.VMEM((ROWS_OWN + 8, 128), F32),
                pltpu.VMEM((ROWS_OWN + 8, 128), F32),
            ],
        ),
        out_shape=jax.ShapeDtypeStruct((TAB_OWN, D, ROWS_DEV), F32),
        compiler_params=params(("arbitrary",)),
    )(landing, arrived)


def send_side(
    event_embed, target, pooled_grad, event_table, event_row, table_slot, lengths, caps,
    w_first, b_first, w_second, b_second, w_score,
):
    table = event_table.transpose(1, 0, 2).reshape(PAIRS, LMAX)
    row = event_row.transpose(1, 0, 2).reshape(PAIRS, LMAX)
    slots, place = find_slots(lengths, caps, table, row, table_slot.reshape(1, -1))
    return pack_grads(
        slots.reshape(-1),
        event_embed.transpose(0, 1, 3, 2),
        target.transpose(1, 0, 2),
        pooled_grad.transpose(1, 0, 2),
        w_first.transpose(0, 2, 1),
        b_first,
        w_second.transpose(0, 2, 1),
        b_second,
        w_score,
        place,
    )


def receive_side(arrived):
    landing = find_landing(arrived)
    summed = add_rows(landing.reshape(-1), arrived.reshape(DEVS * HALF, 128))
    return summed.transpose(0, 2, 1)


def per_device(*args):
    packed = send_side(*args)
    arrived = lax.all_to_all(packed, ("group", "local"), split_axis=0, concat_axis=0, tiled=True)
    return receive_side(arrived)


def solution(mesh):
    split_all = ("group", "local")
    in_specs = (
        P(split_all, None, None, None),
        P(split_all, None, None),
        P(split_all, None, None),
        P(split_all, None, None),
        P(split_all, None, None),
        P(),
        P(split_all, None),
        P(),
        P(),
        P(),
        P(),
        P(),
        P(),
    )
    return jax.shard_map(
        per_device, mesh=mesh, in_specs=in_specs, out_specs=P("group", "local", None), check_vma=False
    )
```

time: 534 us -> 208 us (0.39); the launches traced: 527 us -> 207 us
  local copies, waits for them, and re-layouts: 172 us -> 0 us
  waiting for transfers between devices: 141 us -> 0 us
  other arithmetic: 140 us -> 0 us
  blocking collectives: 0 us -> 115 us
  Pallas kernels: 0 us -> 91.7 us
  matrix products: 40.3 us -> 0 us
  starting transfers between devices: 33 us -> 0 us
    all_to_all x4 -> x0, waiting for transfers between devices: 141 us -> none  [the longest x1 86.6 us: per_device(): lax.all_to_all(halfway[0], 'local', split_axis=1, concat_axis=1, tiled=True)]
    all_to_all x0 -> x1, blocking collectives: none -> 115 us  [per_device(): lax.all_to_all(packed, ('group', 'local'), split_axis=0, concat_axis=0, t...]
    pallas_call x0 -> x4, Pallas kernels: none -> 91.7 us  [the longest x1 47.3 us: pack_grads(): pl.pallas_call(grad_kernel, grid_spec=pltpu.PrefetchScalarGridSpec(num_sc...]
    scatter-add x1 -> x0, other arithmetic: 87.3 us -> none  [per_device(): jnp.zeros((total_rows, width), jnp.float32).at[landing].add(flat_arrived)]
    scatter x2 -> x0, local copies, waits for them, and re-layouts: 67.4 us -> none  [the longest x1 38 us: per_device(): jnp.zeros((buffer_len,), jnp.float32).at[buffer_index].set(row_place)]
    reshape x10 -> x0, local copies, waits for them, and re-layouts: 46.5 us -> none  [the longest x2 21.6 us: per_device(): outgoing = packed_grads.reshape(groups, locals_count, capacity, width)]
    unnamed x36 -> x0, local copies, waits for them, and re-layouts: 45.7 us -> none
    dot_general x7 -> x0, matrix products: 40.3 us -> none  [the longest x1 15.5 us: event_grads(): jnp.einsum('nftk,fkh->nfth', joined, w_first, precision=hp)]
  transfers between devices with their start and end apart: 4 -> 0, of which waited for: 2 -> 0; matrix products, arithmetic and copies ran while one was open for 32% -> 0% of each run, Pallas kernels for 0% -> 0%
where the time goes in v1:
time: 208 us; the launch traced here: 207 us
  blocking collectives  115 us (55%)
  Pallas kernels  91.7 us (44%)
    all_to_all x1, blocking collectives, per_device(): lax.all_to_all(packed, ('group', 'local'), split_axis=0, concat_axis=0, t...  115 us
    pallas_call x1, Pallas kernels, pack_grads(): pl.pallas_call(grad_kernel, grid_spec=pltpu.PrefetchScalarGridSpec(num_sc...  47.3 us
    pallas_call x1, Pallas kernels, add_rows(): pl.pallas_call(add_kernel, grid_spec=pltpu.PrefetchScalarGridSpec(num_sca...  25.2 us
    pallas_call x1, Pallas kernels, find_slots(): pl.pallas_call(index_kernel, in_specs=[smem, smem, vmem, vmem, vmem], out...  16.2 us

profile of v1, /device:TPU:1, one launch (start us, length us, event | category | flops | bytes accessed | tf_op | source)
XLA Modules:
  0.0 207.1 jit_solution(5847879986186803753)
XLA Ops:
  0.0 16.2 %shard_map.127 = (s32[80,128]{1,0:T(8,128)}, f32[256,128]{1,0:T(8,128)}) custom-call(s32[4,20]{1,0:T(4,128)} %len_ref.1, s32[20]{0:T(128)} %cap_ref.1, s32[80,128]{1,0:T(8,128)} %bitcast.22, s32[80,128]{1,0:T(8,128)} %bitcast.23, s32[1,128]{1,0:T(1,128)} %bitcast.26), custom_call_target="tpu_custom_call" | custom-call | tf_op jit(solution)/shard_map/pallas_call | solution.py:276
  16.2 47.3 %shard_map.128 = f32[256,32,128]{2,1,0:T(8,128)} custom-call(s32[10240]{0:T(1024)} %bitcast.21, bf16[4,20,64,128]{3,2,1,0:T(8,128)(2,1)} %bitcast.18, bf16[20,4,64]{2,1,0:T(4,128)(2,1)} %bitcast.24, bf16[20,4,64]{2,1,0:T(4,128)(2,1)} %bitcast.25, f32[20,80,256]{2,1,0:T(8,128)} %bitcast.17, f32[20,80]{1,0:T(8,128)} %b1_ref.1, f32[20,40,80]{2,1,0:T(8,128)} %bitcast.20, ...), custom_call_target="tpu_custom_call" | custom-call | tf_op jit(solution)/shard_map/pallas_call | solution.py:295
  63.5 115.4 %all_to_all.5.tail_ref = f32[256,32,128]{2,1,0:T(8,128)} all-to-all(f32[256,32,128]{2,1,0:T(8,128)} %shard_map.128), channel_id=1, replica_groups=mesh['group'=16,'local'=16] {'group','local'}, dimensions={0} | all-to-all | bytes 8388608 | tf_op jit(solution)/shard_map/all_to_all | solution.py:380
  179.0 2.9 %shard_map.129 = s32[256,128]{1,0:T(8,128)} custom-call(f32[256,32,128]{2,1,0:T(8,128)} %all_to_all.5.tail_ref), custom_call_target="tpu_custom_call" | custom-call | tf_op jit(solution)/shard_map/pallas_call | solution.py:323
  181.9 25.2 %shard_map.130 = f32[8,64,1024]{2,1,0:T(8,128)} custom-call(s32[32768]{0:T(1024)} %bitcast.19, f32[8192,128]{1,0:T(8,128)} %bitcast.16), custom_call_target="tpu_custom_call" | custom-call | tf_op jit(solution)/shard_map/pallas_call | solution.py:334

commit v2 on v1

v2 whole, which is shorter than its diff:
```python
import functools

import jax
import jax.numpy as jnp
from jax import lax
from jax.experimental import pallas as pl
from jax.experimental.pallas import tpu as pltpu
from jax.sharding import PartitionSpec as P

D = 64
F = 20
H1 = 80
H2 = 40
H2_PAD = 48
STEP = 2
RANK_STEP = 4
ADD_STEP = 4
CHUNK = 32
LMAX = 128
B_DEV = 4
TAB_OWN = 8
ROWS_DEV = 1024
GROUPS = 16
LOCALS = 16
DEVS = GROUPS * LOCALS
PAIRS = B_DEV * F
ROWS_OWN = TAB_OWN * ROWS_DEV
BUCKET = 64
HALF = 32
DUMMY = DEVS * BUCKET
BF = jnp.bfloat16
F32 = jnp.float32
VMEM_BYTES = 56 * 1024 * 1024


def dot(left, right, contract=((1,), (0,))):
    return lax.dot_general(
        left, right, (contract, ((), ())), preferred_element_type=F32
    )


def index_kernel(len_ref, cap_ref, table_ref, row_ref, places_ref, slots_ref, out_ref, dev_ref, own_ref, carry_ref):
    table = table_ref[...]
    place = jnp.take_along_axis(
        jnp.broadcast_to(places_ref[...], table.shape), table, axis=1, mode="promise_in_bounds"
    )
    row = row_ref[...]
    dev_ref[...] = (place >> 3) * LOCALS + (row >> 10)
    own_ref[...] = (place & 7) * ROWS_DEV + (row & 1023)
    carry_ref[...] = jnp.zeros_like(carry_ref)
    out_ref[...] = jnp.zeros_like(out_ref)
    span = B_DEV * LMAX
    lane = lax.broadcasted_iota(jnp.int32, (1, LMAX), 1)
    dev_iota = lax.broadcasted_iota(jnp.int32, (DEVS, LMAX), 0)
    tri_row = lax.broadcasted_iota(jnp.int32, (span, span + LMAX), 0)
    tri_col = lax.broadcasted_iota(jnp.int32, (span, span + LMAX), 1)
    earlier = (tri_row < tri_col).astype(F32).astype(BF)
    pos_iota = lax.broadcasted_iota(jnp.int32, (BUCKET, LMAX), 0)

    def features(i, _):
        hits, counts, hots, owns, keeps, devs = [], [], [], [], [], []
        for k in range(RANK_STEP):
            f = i * RANK_STEP + k
            for n in range(B_DEV):
                p = f * B_DEV + n
                kept = lane < jnp.minimum(len_ref[n, f], cap_ref[f])
                dev = dev_ref[pl.ds(p, 1), :]
                keeps.append(kept)
                devs.append(dev)
                owns.append(own_ref[pl.ds(p, 1), :])
                hits.append(dev_iota == jnp.where(kept, dev, -1))
            hot = jnp.concatenate(
                [jnp.where(hits[k * B_DEV + n], 1.0, 0.0).astype(BF) for n in range(B_DEV)], axis=1
            )
            hots.append(hot)
            counts.append(dot(hot, earlier))
        carry = carry_ref[...]
        total = out_ref[...]
        for k in range(RANK_STEP):
            spreads = []
            for n in range(B_DEV):
                at = k * B_DEV + n
                before = counts[k][:, n * LMAX : (n + 1) * LMAX] + carry
                pos = jnp.sum(jnp.where(hits[at], before, 0.0), axis=0, keepdims=True)
                pos = pos.astype(jnp.int32)
                slot = devs[at] * BUCKET + (pos & 1) * HALF + (pos >> 1)
                slots_ref[pl.ds(i * (RANK_STEP * B_DEV) + at, 1), :] = jnp.where(
                    keeps[at], slot, DUMMY
                )
                high = ((owns[at] >> 7) + 1).astype(F32)
                low = (owns[at] & 127).astype(F32)
                same = pos_iota == pos
                spreads.append(
                    jnp.concatenate(
                        [jnp.where(same, high, 0.0).astype(BF), jnp.where(same, low, 0.0).astype(BF)],
                        axis=0,
                    )
                )
            total = total + dot(hots[k], jnp.concatenate(spreads, axis=1), ((1,), (1,)))
            carry = carry + counts[k][:, span:]
        carry_ref[...] = carry
        out_ref[...] = total
        return 0

    lax.fori_loop(0, F // RANK_STEP, features, 0)
    parts = out_ref[...]
    high = pltpu.roll(parts, BUCKET, 1)
    out_ref[...] = jnp.where(high > 0.0, high * 128.0 + parts - 128.0, float(ROWS_OWN))


def to_column(row, size):
    rows = lax.broadcasted_iota(jnp.int32, (size, row.shape[1]), 0)
    cols = lax.broadcasted_iota(jnp.int32, (size, row.shape[1]), 1)
    return jnp.where(rows == cols, row, 0.0)


def split(value):
    high = value.astype(BF)
    low = (value - high.astype(F32)).astype(BF)
    return high, low


def grad_kernel(
    slots_ref,
    event_ref,
    query_ref,
    up_ref,
    w1_ref,
    b1_ref,
    w2_ref,
    b2_ref,
    ws_ref,
    place_ref,
    out_ref,
    bucket_ref,
    grad_ref,
    pack_ref,
    sems,
):
    step = pl.program_id(0)

    def scatter(base):
        for t in range(STEP * B_DEV * LMAX):
            slot = slots_ref[base + t]
            bucket_ref[pl.ds(slot, 1), :] = grad_ref[t : t + 1, :]

    scatter(jnp.maximum(step - 1, 0) * (STEP * B_DEV * LMAX))
    left_half = lax.broadcasted_iota(jnp.int32, (H1, 128), 1) < D
    row_at = lax.broadcasted_iota(jnp.int32, (16, 128), 0)
    lane_at = lax.broadcasted_iota(jnp.int32, (16, 128), 1)
    folds, ups, pre1, dscore, b2, ws, w2t_all, w2_all = ([] for _ in range(8))
    for k in range(STEP):
        f = step * STEP + k
        w1 = w1_ref[k]
        wa, wb, wc, wd = (w1[:, i * D : (i + 1) * D] for i in range(4))
        wad = wa + wd
        wbd = wb - wd
        wad = jnp.concatenate([wad, wad], axis=1)
        wcc = jnp.concatenate([wc, wc], axis=1)
        wbd = jnp.concatenate([wbd, jnp.zeros((H1, D), F32)], axis=1)
        b1_diag = to_column(
            jnp.concatenate([b1_ref[pl.ds(f, 1), :], jnp.zeros((1, 128 - H1), F32)], axis=1), H1
        )
        b2.append(jnp.sum(to_column(b2_ref[pl.ds(f, 1), :], H2_PAD), axis=1, keepdims=True))
        ws.append(jnp.sum(to_column(ws_ref[pl.ds(f, 1), :], H2_PAD), axis=1, keepdims=True))
        w2t = jnp.concatenate([w2_ref[k], jnp.zeros((H2_PAD - H2, H1), F32)], axis=0)
        w2t_hi, w2t_lo = split(w2t)
        w2_hi, w2_lo = split(w2t.T)
        w2t_all.append(jnp.concatenate([w2t_hi, w2t_lo, w2t_hi], axis=1))
        w2_all.append(jnp.concatenate([w2_hi, w2_lo, w2_hi], axis=1))
        firsts = []
        for n in range(B_DEV):
            events = event_ref[n, k]
            query = query_ref[k, n : n + 1, :].astype(F32)
            up = up_ref[k, n : n + 1, :].astype(F32)
            query = jnp.concatenate([query, query], axis=1)
            up = jnp.concatenate([up, up], axis=1)
            folded = wad + wcc * query
            fold_hi = folded.astype(BF)
            fold_rest = folded - fold_hi.astype(F32)
            offset = jnp.sum(wbd * query + b1_diag, axis=1, keepdims=True)
            both = jnp.where(left_half, fold_hi.astype(F32), fold_rest).astype(BF)
            up_row = jnp.where((row_at == 0) & (lane_at < D), up, 0.0).astype(BF)
            first = dot(
                jnp.concatenate([both, up_row], axis=0), jnp.concatenate([events, events], axis=0)
            )
            firsts.append((first[:H1] + offset, first[H1 : H1 + 1]))
            folds.append((fold_hi, fold_rest.astype(BF)))
            ups.append(jnp.where(row_at < 2, up, 0.0).astype(BF))
        pre1.append(jnp.concatenate([first[0] for first in firsts], axis=1))
        dscore.append(jnp.concatenate([first[1] for first in firsts], axis=1))
    pre2, slope1, score, d1 = [], [], [], []
    for k in range(STEP):
        sig1 = 0.5 + 0.5 * jnp.tanh(0.5 * pre1[k])
        h1 = pre1[k] * sig1
        slope1.append(sig1 + h1 * (1.0 - sig1))
        h1_hi, h1_lo = split(h1)
        pre2.append(dot(w2t_all[k], jnp.concatenate([h1_hi, h1_hi, h1_lo], axis=0)) + b2[k])
    for k in range(STEP):
        sig2 = 0.5 + 0.5 * jnp.tanh(0.5 * pre2[k])
        h2 = pre2[k] * sig2
        slope2 = sig2 + h2 * (1.0 - sig2)
        score.append(jnp.sum(h2 * ws[k], axis=0, keepdims=True))
        d2_hi, d2_lo = split((dscore[k] * ws[k]) * slope2)
        d1.append(dot(w2_all[k], jnp.concatenate([d2_hi, d2_hi, d2_lo], axis=0)))
    for k in range(STEP):
        d1_hi, d1_lo = split(d1[k] * slope1[k])
        score_hi = score[k].astype(BF).astype(F32)
        score_lo = score[k] - score_hi
        for n in range(B_DEV):
            at = slice(n * LMAX, (n + 1) * LMAX)
            score_rows = jnp.where(
                row_at == 0, score_hi[:, at], jnp.where(row_at == 1, score_lo[:, at], 0.0)
            ).astype(BF)
            fold_hi, fold_lo = folds[k * B_DEV + n]
            row = (k * B_DEV + n) * LMAX
            grad_ref[row : row + LMAX, :] = dot(
                jnp.concatenate([d1_hi[:, at], d1_lo[:, at], d1_hi[:, at], score_rows], axis=0),
                jnp.concatenate([fold_hi, fold_hi, fold_lo, ups[k * B_DEV + n]], axis=0),
                ((0,), (0,)),
            )

    @pl.when(step == F // STEP - 1)
    def _():
        scatter(step * (STEP * B_DEV * LMAX))
        lanes = lax.broadcasted_iota(jnp.int32, (HALF, 128), 1) < D

        def pack(chunk, _):
            def one(k, _):
                dev = chunk * CHUNK + k
                at = pl.multiple_of(dev * BUCKET, BUCKET)
                bucket_ref[pl.ds(at + BUCKET - 1, 1), :] = place_ref[pl.ds(dev, 1), :]
                left = bucket_ref[pl.ds(at, HALF), :]
                right = bucket_ref[pl.ds(pl.multiple_of(at + HALF, HALF), HALF), :]
                pack_ref[dev] = jnp.where(lanes, left, right)
                return 0

            lax.fori_loop(0, CHUNK, one, 0, unroll=8)
            part = pl.ds(chunk * CHUNK, CHUNK)
            pltpu.make_async_copy(pack_ref.at[part], out_ref.at[part], sems.at[chunk]).start()
            return 0

        def finish(chunk, _):
            part = pl.ds(chunk * CHUNK, CHUNK)
            pltpu.make_async_copy(pack_ref.at[part], out_ref.at[part], sems.at[chunk]).wait()
            return 0

        lax.fori_loop(0, DEVS // CHUNK, pack, 0)
        lax.fori_loop(0, DEVS // CHUNK, finish, 0)


def add_kernel(in_ref, out_ref, new_ref, tail_ref, spot_ref, land_ref, turn_ref, sems, *sums):
    whole = pltpu.make_async_copy(in_ref, new_ref, sems.at[0])
    tails = pltpu.make_async_copy(in_ref.at[:, HALF - 8 :, :], tail_ref, sems.at[1])
    tails.start()
    whole.start()

    def clear(i, _):
        at = pl.multiple_of(i * 64, 64)
        for total in sums:
            total[pl.ds(at, 64), :] = jnp.zeros((64, 128), F32)
        return 0

    lax.fori_loop(0, ROWS_OWN // 64, clear, 0)
    tails.wait()
    values = tail_ref[:, 7, :].astype(jnp.int32)
    lane = lax.broadcasted_iota(jnp.int32, values.shape, 1)
    filled = (lane >= D) & (values < ROWS_OWN)
    count = jnp.sum(filled.astype(jnp.int32), axis=1, keepdims=True)
    clash = jnp.zeros(values.shape, jnp.int32)
    for shift in range(2, 16, 2):
        moved = pltpu.roll(values, shift, 1)
        same = filled & (moved == values) & ((lane & 15) >= shift)
        clash = clash | same.astype(jnp.int32)
    clashes = jnp.sum(clash, axis=1, keepdims=True)
    later = pltpu.roll(jnp.where(clash > 0, values, ROWS_OWN), D, 1)
    spots = jnp.where(lane < D, later, jnp.where(clash > 0, ROWS_OWN, values))
    mode = jnp.where(count > 32, 1, 0) + jnp.where(clashes > 0, 2, 0)
    spots = jnp.where(lane == 60, mode, jnp.where(lane == 61, count, spots))
    spot_ref[...] = spots
    spots = pltpu.make_async_copy(spot_ref, land_ref, sems.at[2])
    spots.start()
    spots.wait()
    whole.wait()

    def batch(s, start):
        parts = []
        for b in range(2):
            row = start + b * 8
            for side in range(2):
                total = sums[2 * b + side]
                at = [land_ref[s, D + 2 * (row + j) + side] for j in range(8)]
                add = [
                    total[pl.ds(at[j], 1), :] + new_ref[s, pl.ds(row + j, 1), :] for j in range(8)
                ]
                parts.append((total, at, add))
        for total, at, add in parts:
            for j in range(8):
                total[pl.ds(at[j], 1), :] = add[j]

    def sources(i, _):
        for k in range(ADD_STEP):
            batch(i * ADD_STEP + k, 0)
        for k in range(ADD_STEP):
            s = i * ADD_STEP + k
            mode = land_ref[s, 60]

            @pl.when(mode > 0)
            def _():
                @pl.when((mode & 1) == 1)
                def _():
                    batch(s, 16)

                @pl.when(mode >= 2)
                def _():
                    def single(j, _):
                        new = new_ref[s, pl.ds(j, 1), :]
                        for side in range(2):
                            sums[side][pl.ds(land_ref[s, 2 * j + side], 1), :] += new
                        return 0

                    lax.fori_loop(0, (land_ref[s, 61] + 1) >> 1, single, 0)

        return 0

    lax.fori_loop(0, DEVS // ADD_STEP, sources, 0)
    lanes = lax.broadcasted_iota(jnp.int32, (128, 128), 1) < D
    for table in range(TAB_OWN):
        for block in range(ROWS_DEV // 128):
            at = table * ROWS_DEV + block * 128
            at = slice(at, at + 128)
            joined = jnp.where(
                lanes, sums[0][at, :] + sums[2][at, :], sums[1][at, :] + sums[3][at, :]
            )
            turned = joined.T
            turn_ref[table, :, block * 128 : (block + 1) * 128] = turned[:D] + turned[D:]
        pltpu.make_async_copy(turn_ref.at[table], out_ref.at[table], sems.at[3 + table]).start()
    for table in range(TAB_OWN):
        pltpu.make_async_copy(turn_ref.at[table], out_ref.at[table], sems.at[3 + table]).wait()


def params(semantics=None):
    return pltpu.CompilerParams(vmem_limit_bytes=VMEM_BYTES, dimension_semantics=semantics)


def find_slots(lengths, caps, table, row, places):
    smem = pl.BlockSpec(memory_space=pltpu.SMEM)
    vmem = pl.BlockSpec(memory_space=pltpu.VMEM)
    return pl.pallas_call(
        index_kernel,
        in_specs=[smem, smem, vmem, vmem, vmem],
        out_specs=[vmem, vmem],
        out_shape=[
            jax.ShapeDtypeStruct((PAIRS, LMAX), jnp.int32),
            jax.ShapeDtypeStruct((DEVS, LMAX), F32),
        ],
        scratch_shapes=[
            pltpu.VMEM((PAIRS, LMAX), jnp.int32),
            pltpu.VMEM((PAIRS, LMAX), jnp.int32),
            pltpu.VMEM((DEVS, LMAX), F32),
        ],
        compiler_params=params(),
    )(lengths, caps, table, row, places)


def pack_grads(slots, events, query, up, w1, b1, w2, b2, ws, place):
    whole = lambda shape: pl.BlockSpec(shape, lambda f, s: (0,) * len(shape))
    return pl.pallas_call(
        grad_kernel,
        grid_spec=pltpu.PrefetchScalarGridSpec(
            num_scalar_prefetch=1,
            grid=(F // STEP,),
            in_specs=[
                pl.BlockSpec((B_DEV, STEP, D, LMAX), lambda f, s: (0, f, 0, 0)),
                pl.BlockSpec((STEP, B_DEV, D), lambda f, s: (f, 0, 0)),
                pl.BlockSpec((STEP, B_DEV, D), lambda f, s: (f, 0, 0)),
                pl.BlockSpec((STEP, H1, 4 * D), lambda f, s: (f, 0, 0)),
                whole((F, H1)),
                pl.BlockSpec((STEP, H2, H1), lambda f, s: (f, 0, 0)),
                whole((F, H2)),
                whole((F, H2)),
                whole((DEVS, LMAX)),
            ],
            out_specs=pl.BlockSpec(memory_space=pl.ANY),
            scratch_shapes=[
                pltpu.VMEM((DUMMY + 8, 128), F32),
                pltpu.VMEM((STEP * B_DEV * LMAX, 128), F32),
                pltpu.VMEM((DEVS, HALF, 128), F32),
                pltpu.SemaphoreType.DMA((DEVS // CHUNK,)),
            ],
        ),
        out_shape=jax.ShapeDtypeStruct((DEVS, HALF, 128), F32),
        compiler_params=params(("arbitrary",)),
    )(slots, events, query, up, w1, b1, w2, b2, ws, place)


def add_rows(arrived):
    return pl.pallas_call(
        add_kernel,
        in_specs=[pl.BlockSpec(memory_space=pl.ANY)],
        out_specs=pl.BlockSpec(memory_space=pl.ANY),
        out_shape=jax.ShapeDtypeStruct((TAB_OWN, D, ROWS_DEV), F32),
        scratch_shapes=[
            pltpu.VMEM((DEVS, HALF, 128), F32),
            pltpu.VMEM((DEVS, 8, 128), F32),
            pltpu.VMEM((DEVS, 128), jnp.int32),
            pltpu.SMEM((DEVS, 128), jnp.int32),
            pltpu.VMEM((TAB_OWN, D, ROWS_DEV), F32),
            pltpu.SemaphoreType.DMA((3 + TAB_OWN,)),
        ]
        + [pltpu.VMEM((ROWS_OWN + 8, 128), F32)] * 4,
        compiler_params=params(),
    )(arrived)


def send_side(
    event_embed, target, pooled_grad, event_table, event_row, table_slot, lengths, caps,
    w_first, b_first, w_second, b_second, w_score,
):
    table = event_table.transpose(1, 0, 2).reshape(PAIRS, LMAX)
    row = event_row.transpose(1, 0, 2).reshape(PAIRS, LMAX)
    slots, place = find_slots(lengths, caps, table, row, table_slot.reshape(1, -1))
    return pack_grads(
        slots.reshape(-1),
        event_embed.transpose(0, 1, 3, 2),
        target.transpose(1, 0, 2),
        pooled_grad.transpose(1, 0, 2),
        w_first.transpose(0, 2, 1),
        b_first,
        w_second.transpose(0, 2, 1),
        b_second,
        w_score,
        place,
    )


def receive_side(arrived):
    return add_rows(arrived).transpose(0, 2, 1)


def per_device(*args):
    packed = send_side(*args)
    arrived = lax.all_to_all(packed, ("group", "local"), split_axis=0, concat_axis=0, tiled=True)
    return receive_side(arrived)


def solution(mesh):
    split_all = ("group", "local")
    in_specs = (
        P(split_all, None, None, None),
        P(split_all, None, None),
        P(split_all, None, None),
        P(split_all, None, None),
        P(split_all, None, None),
        P(),
        P(split_all, None),
        P(),
        P(),
        P(),
        P(),
        P(),
        P(),
    )
    return jax.shard_map(
        per_device, mesh=mesh, in_specs=in_specs, out_specs=P("group", "local", None), check_vma=False
    )
```

time: 208 us -> 168 us (0.81)
  Pallas kernels: 91.7 us -> 51.7 us
    pallas_call x1, Pallas kernels: 47.3 us -> 23.5 us  [pack_grads(): pl.pallas_call(grad_kernel, grid_spec=pltpu.PrefetchScalarGridSpec(num_sc...]
    pallas_call x2 -> x1, Pallas kernels: 28.2 us -> 19.3 us  [add_rows(): pl.pallas_call(add_kernel, in_specs=[pl.BlockSpec(memory_space=pl.ANY)],...]
    pallas_call x1, Pallas kernels: 16.2 us -> 8.96 us  [find_slots(): pl.pallas_call(index_kernel, in_specs=[smem, smem, vmem, vmem, vmem], out...]
where the time goes in v2:
time: 168 us; the launch traced here: 167 us
  blocking collectives  115 us (68%)
  Pallas kernels  51.7 us (31%)
    all_to_all x1, blocking collectives, per_device(): lax.all_to_all(packed, ('group', 'local'), split_axis=0, concat_axis=0, t...  115 us
    pallas_call x1, Pallas kernels, pack_grads(): pl.pallas_call(grad_kernel, grid_spec=pltpu.PrefetchScalarGridSpec(num_sc...  23.5 us
    pallas_call x1, Pallas kernels, add_rows(): pl.pallas_call(add_kernel, in_specs=[pl.BlockSpec(memory_space=pl.ANY)],...  19.3 us
    pallas_call x1, Pallas kernels, find_slots(): pl.pallas_call(index_kernel, in_specs=[smem, smem, vmem, vmem, vmem], out...  8.96 us

profile of v2, /device:TPU:1, one launch (start us, length us, event | category | flops | bytes accessed | tf_op | source)
XLA Modules:
  0.0 167.2 jit_solution(3872990897827366352)
XLA Ops:
  0.0 9.0 %shard_map.127 = (s32[80,128]{1,0:T(8,128)}, f32[256,128]{1,0:T(8,128)}) custom-call(s32[4,20]{1,0:T(4,128)} %len_ref.1, s32[20]{0:T(128)} %cap_ref.1, s32[80,128]{1,0:T(8,128)} %bitcast.18, s32[80,128]{1,0:T(8,128)} %bitcast.19, s32[1,128]{1,0:T(1,128)} %bitcast.22), custom_call_target="tpu_custom_call" | custom-call | tf_op jit(solution)/shard_map/pallas_call | solution.py:349
  9.0 23.5 %shard_map.128 = f32[256,32,128]{2,1,0:T(8,128)} custom-call(s32[10240]{0:T(1024)} %bitcast.17, bf16[4,20,64,128]{3,2,1,0:T(8,128)(2,1)} %bitcast.15, bf16[20,4,64]{2,1,0:T(4,128)(2,1)} %bitcast.20, bf16[20,4,64]{2,1,0:T(4,128)(2,1)} %bitcast.21, f32[20,80,256]{2,1,0:T(8,128)} %bitcast.14, f32[20,80]{1,0:T(8,128)} %b1_ref.1, f32[20,40,80]{2,1,0:T(8,128)} %bitcast.16, ...), custom_call_target="tpu_custom_call" | custom-call | tf_op jit(solution)/shard_map/pallas_call | solution.py:368
  32.4 115.4 %all_to_all.5.in_ref = f32[256,32,128]{2,1,0:T(8,128)} all-to-all(f32[256,32,128]{2,1,0:T(8,128)} %shard_map.128), channel_id=1, replica_groups=mesh['group'=16,'local'=16] {'group','local'}, dimensions={0} | all-to-all | bytes 8388608 | tf_op jit(solution)/shard_map/all_to_all | solution.py:443
  147.9 19.3 %shard_map.129 = f32[8,64,1024]{2,1,0:T(8,128)} custom-call(f32[256,32,128]{2,1,0:T(8,128)} %all_to_all.5.in_ref), custom_call_target="tpu_custom_call" | custom-call | tf_op jit(solution)/shard_map/pallas_call | solution.py:398

commit v3 on v2

v3 whole, which is shorter than its diff:
```python
import functools

import jax
import jax.numpy as jnp
from jax import lax
from jax.experimental import pallas as pl
from jax.experimental.pallas import tpu as pltpu
from jax.sharding import PartitionSpec as P

D = 64
F = 20
H1 = 80
H2 = 40
H2_PAD = 48
LMAX = 128
B_DEV = 4
TAB_OWN = 8
ROWS_DEV = 1024
LOCALS = 16
DEVS = 256
PAIRS = B_DEV * F
ROWS_OWN = TAB_OWN * ROWS_DEV
STEP = 2
STEPS = F // STEP
SPAN = STEP * B_DEV
EVENTS = SPAN * LMAX
BLOCK = 2 * LMAX
BUCKET = 64
HALF = 32
ROWS = 28
MAIN = 2 * ROWS - 1
LATE = HALF - ROWS
PLACES = 60
DUMMY = DEVS * BUCKET
CHUNK = 32
PIECES = 4
PIECE = DEVS // PIECES
ADD_STEP = 4
BF = jnp.bfloat16
F32 = jnp.float32
VMEM_BYTES = 63 * 1024 * 1024


def dot(left, right, contract=((1,), (0,))):
    return lax.dot_general(left, right, (contract, ((), ())), preferred_element_type=F32)


def diagonal(row, size):
    rows = lax.broadcasted_iota(jnp.int32, (size, row.shape[1]), 0)
    cols = lax.broadcasted_iota(jnp.int32, (size, row.shape[1]), 1)
    return jnp.where(rows == cols, row, 0.0)


def split(value):
    high = value.astype(BF)
    low = (value - high.astype(F32)).astype(BF)
    return high, low


def rank_events(step, len_ref, cap_ref, table_ref, row_ref, places_ref, earlier_ref, carry_ref, place_ref, slots_ref):
    table = table_ref[...]
    place = jnp.take_along_axis(
        jnp.broadcast_to(places_ref[...], table.shape), table, axis=1, mode="promise_in_bounds"
    )
    row = row_ref[...]
    devs = (place >> 3) * LOCALS + (row >> 10)
    owns = (place & 7) * ROWS_DEV + (row & 1023)
    highs = ((owns >> 7) + 1).astype(F32)
    lows = (owns & 127).astype(F32)
    lane = lax.broadcasted_iota(jnp.int32, (1, LMAX), 1)
    dev_iota = lax.broadcasted_iota(jnp.int32, (DEVS, LMAX), 0)
    pos_iota = lax.broadcasted_iota(jnp.int32, (BUCKET, LMAX), 0)
    keeps, hits, hots, counts = [], [], [], []
    for p in range(SPAN):
        f = step * STEP + p // B_DEV
        kept = lane < jnp.minimum(len_ref[p % B_DEV, f], cap_ref[f])
        keeps.append(kept)
        hits.append(dev_iota == jnp.where(kept, devs[p : p + 1], -1))
    for p in range(0, SPAN, 2):
        hot = jnp.concatenate(
            [jnp.where(hits[p + k], 1.0, 0.0).astype(BF) for k in range(2)], axis=1
        )
        hots.append(hot)
        counts.append(dot(hot, earlier_ref[...]))
    carry = carry_ref[...]
    total = place_ref[...]
    for b in range(SPAN // 2):
        spreads = []
        for k in range(2):
            p = 2 * b + k
            before = counts[b][:, k * LMAX : (k + 1) * LMAX] + carry
            pos = jnp.sum(jnp.where(hits[p], before, 0.0), axis=0, keepdims=True).astype(jnp.int32)
            spot = jnp.where(pos >= MAIN, pos + 1, pos)
            slot = devs[p : p + 1] * BUCKET + (spot & 1) * HALF + (spot >> 1)
            slots_ref[p : p + 1, :] = jnp.where(keeps[p], slot, DUMMY)
            same = pos_iota == pos
            spreads.append(
                jnp.concatenate(
                    [
                        jnp.where(same, highs[p : p + 1], 0.0).astype(BF),
                        jnp.where(same, lows[p : p + 1], 0.0).astype(BF),
                    ],
                    axis=0,
                )
            )
        total = total + dot(hots[b], jnp.concatenate(spreads, axis=1), ((1,), (1,)))
        carry = carry + counts[b][:, BLOCK:]
    carry_ref[...] = carry
    place_ref[...] = total


def event_grads(step, event_ref, query_ref, up_ref, w1_ref, b1_ref, w2_ref, b2_ref, ws_ref, grad_ref):
    left_half = lax.broadcasted_iota(jnp.int32, (H1, 128), 1) < D
    row_at = lax.broadcasted_iota(jnp.int32, (16, 128), 0)
    lane_at = lax.broadcasted_iota(jnp.int32, (16, 128), 1)
    folds, ups, pre1, dscore, b2, ws, w2t_all, w2_all = ([] for _ in range(8))
    for k in range(STEP):
        f = step * STEP + k
        w1 = w1_ref[k]
        wa, wb, wc, wd = (w1[:, i * D : (i + 1) * D] for i in range(4))
        wad = wa + wd
        wbd = wb - wd
        wad = jnp.concatenate([wad, wad], axis=1)
        wcc = jnp.concatenate([wc, wc], axis=1)
        wbd = jnp.concatenate([wbd, jnp.zeros((H1, D), F32)], axis=1)
        b1_diag = diagonal(
            jnp.concatenate([b1_ref[pl.ds(f, 1), :], jnp.zeros((1, 128 - H1), F32)], axis=1), H1
        )
        b2.append(jnp.sum(diagonal(b2_ref[pl.ds(f, 1), :], H2_PAD), axis=1, keepdims=True))
        ws.append(jnp.sum(diagonal(ws_ref[pl.ds(f, 1), :], H2_PAD), axis=1, keepdims=True))
        w2t = jnp.concatenate([w2_ref[k], jnp.zeros((H2_PAD - H2, H1), F32)], axis=0)
        w2t_hi, w2t_lo = split(w2t)
        w2_hi, w2_lo = split(w2t.T)
        w2t_all.append(jnp.concatenate([w2t_hi, w2t_lo, w2t_hi], axis=1))
        w2_all.append(jnp.concatenate([w2_hi, w2_lo, w2_hi], axis=1))
        firsts = []
        for n in range(B_DEV):
            events = event_ref[n, k]
            query = query_ref[k, n : n + 1, :].astype(F32)
            up = up_ref[k, n : n + 1, :].astype(F32)
            query = jnp.concatenate([query, query], axis=1)
            up = jnp.concatenate([up, up], axis=1)
            folded = wad + wcc * query
            fold_hi = folded.astype(BF)
            fold_rest = folded - fold_hi.astype(F32)
            offset = jnp.sum(wbd * query + b1_diag, axis=1, keepdims=True)
            both = jnp.where(left_half, fold_hi.astype(F32), fold_rest).astype(BF)
            up_row = jnp.where((row_at == 0) & (lane_at < D), up, 0.0).astype(BF)
            first = dot(
                jnp.concatenate([both, up_row], axis=0), jnp.concatenate([events, events], axis=0)
            )
            firsts.append((first[:H1] + offset, first[H1 : H1 + 1]))
            folds.append((fold_hi, fold_rest.astype(BF)))
            ups.append(jnp.where(row_at < 2, up, 0.0).astype(BF))
        pre1.append(jnp.concatenate([first[0] for first in firsts], axis=1))
        dscore.append(jnp.concatenate([first[1] for first in firsts], axis=1))
    pre2, slope1, score, d1 = [], [], [], []
    for k in range(STEP):
        sig1 = 0.5 + 0.5 * jnp.tanh(0.5 * pre1[k])
        h1 = pre1[k] * sig1
        slope1.append(sig1 + h1 * (1.0 - sig1))
        h1_hi, h1_lo = split(h1)
        pre2.append(dot(w2t_all[k], jnp.concatenate([h1_hi, h1_hi, h1_lo], axis=0)) + b2[k])
    for k in range(STEP):
        sig2 = 0.5 + 0.5 * jnp.tanh(0.5 * pre2[k])
        h2 = pre2[k] * sig2
        slope2 = sig2 + h2 * (1.0 - sig2)
        score.append(jnp.sum(h2 * ws[k], axis=0, keepdims=True))
        d2_hi, d2_lo = split((dscore[k] * ws[k]) * slope2)
        d1.append(dot(w2_all[k], jnp.concatenate([d2_hi, d2_hi, d2_lo], axis=0)))
    for k in range(STEP):
        d1_hi, d1_lo = split(d1[k] * slope1[k])
        score_hi = score[k].astype(BF).astype(F32)
        score_lo = score[k] - score_hi
        for n in range(B_DEV):
            at = slice(n * LMAX, (n + 1) * LMAX)
            score_rows = jnp.where(
                row_at == 0, score_hi[:, at], jnp.where(row_at == 1, score_lo[:, at], 0.0)
            ).astype(BF)
            fold_hi, fold_lo = folds[k * B_DEV + n]
            row = (k * B_DEV + n) * LMAX
            grad_ref[row : row + LMAX, :] = dot(
                jnp.concatenate([d1_hi[:, at], d1_lo[:, at], d1_hi[:, at], score_rows], axis=0),
                jnp.concatenate([fold_hi, fold_hi, fold_lo, ups[k * B_DEV + n]], axis=0),
                ((0,), (0,)),
            )


def send_kernel(
    len_ref,
    cap_ref,
    table_ref,
    row_ref,
    places_ref,
    event_ref,
    query_ref,
    up_ref,
    w1_ref,
    b1_ref,
    w2_ref,
    b2_ref,
    ws_ref,
    main_ref,
    late_ref,
    earlier_ref,
    carry_ref,
    place_ref,
    slots_ref,
    index_ref,
    bucket_ref,
    grad_ref,
    pack_ref,
    rest_ref,
    slot_sem,
    sems,
):
    step = pl.program_id(0)

    def slot_copy():
        return pltpu.make_async_copy(slots_ref, index_ref, slot_sem)

    def scatter():
        for t in range(EVENTS):
            slot = index_ref[t // LMAX, t % LMAX]
            bucket_ref[pl.ds(slot, 1), :] = grad_ref[t : t + 1, :]

    @pl.when(step == 0)
    def _():
        rows = lax.broadcasted_iota(jnp.int32, (BLOCK, BLOCK + LMAX), 0)
        cols = lax.broadcasted_iota(jnp.int32, (BLOCK, BLOCK + LMAX), 1)
        earlier_ref[...] = jnp.where(rows < cols, 1.0, 0.0).astype(BF)
        carry_ref[...] = jnp.zeros_like(carry_ref)
        place_ref[...] = jnp.zeros_like(place_ref)
        slots_ref[...] = jnp.full(slots_ref.shape, DUMMY, jnp.int32)
        slot_copy().start()
        slot_copy().wait()

    scatter()
    rank_events(
        step, len_ref, cap_ref, table_ref, row_ref, places_ref, earlier_ref, carry_ref, place_ref,
        slots_ref,
    )
    event_grads(step, event_ref, query_ref, up_ref, w1_ref, b1_ref, w2_ref, b2_ref, ws_ref, grad_ref)
    slot_copy().start()
    slot_copy().wait()

    @pl.when(step == STEPS - 1)
    def _():
        scatter()
        parts = place_ref[...]
        high = pltpu.roll(parts, BUCKET, 1)
        lane = lax.broadcasted_iota(jnp.int32, parts.shape, 1)
        over = (jnp.max(carry_ref[...]) > float(MAIN)).astype(F32)
        spots = jnp.where(high > 0.0, high * 128.0 + parts - 128.0, float(ROWS_OWN))
        place_ref[...] = jnp.where(lane == 127, over, spots)
        main = pack_ref.reshape(DEVS * ROWS, 128)
        rest = rest_ref.reshape(DEVS * LATE, 128)
        lanes = lax.broadcasted_iota(jnp.int32, (HALF, 128), 1) < D

        def copies(chunk):
            part = pl.ds(chunk * CHUNK, CHUNK)
            return (
                pltpu.make_async_copy(pack_ref.at[part], main_ref.at[part], sems.at[0, chunk]),
                pltpu.make_async_copy(rest_ref.at[part], late_ref.at[part], sems.at[1, chunk]),
            )

        def pack(chunk, _):
            def two(k, _):
                pair = chunk * (CHUNK // 2) + k
                blocks = []
                for side in range(2):
                    dev = pair * 2 + side
                    at = pl.multiple_of(dev * BUCKET, BUCKET)
                    bucket_ref[pl.ds(at + HALF + ROWS - 1, 1), :] = place_ref[pl.ds(dev, 1), :]
                    left = bucket_ref[pl.ds(at, HALF), :]
                    right = bucket_ref[pl.ds(pl.multiple_of(at + HALF, HALF), HALF), :]
                    blocks.append(jnp.where(lanes, left, right))
                at = pl.multiple_of(pair * (2 * ROWS), 2 * ROWS)
                main[pl.ds(at, 2 * ROWS), :] = jnp.concatenate([b[:ROWS] for b in blocks], axis=0)
                at = pl.multiple_of(pair * (2 * LATE), 2 * LATE)
                rest[pl.ds(at, 2 * LATE), :] = jnp.concatenate([b[ROWS:] for b in blocks], axis=0)
                return 0

            lax.fori_loop(0, CHUNK // 2, two, 0, unroll=4)
            for copy in copies(chunk):
                copy.start()
            return 0

        def finish(chunk, _):
            for copy in copies(chunk):
                copy.wait()
            return 0

        lax.fori_loop(0, DEVS // CHUNK, pack, 0)
        lax.fori_loop(0, DEVS // CHUNK, finish, 0)


def add_kernel(in_ref, out_ref, over_ref, late_ref, new_ref, tail_ref, spot_ref, land_ref, turn_ref, sems, *sums):
    def rows_copy(k):
        part = pl.ds(k * PIECE, PIECE)
        return pltpu.make_async_copy(in_ref.at[part], new_ref.at[part], sems.at[1 + k])

    def spots_copy(k):
        part = pl.ds(k * PIECE, PIECE)
        return pltpu.make_async_copy(spot_ref.at[part], land_ref.at[part], sems.at[1 + PIECES + k])

    def table_copy(table):
        done = sems.at[1 + 2 * PIECES + table]
        return pltpu.make_async_copy(turn_ref.at[table], out_ref.at[table], done)

    tails = pltpu.make_async_copy(in_ref.at[:, ROWS - 1], tail_ref, sems.at[0])
    tails.start()
    for k in range(PIECES):
        rows_copy(k).start()

    def clear(i, _):
        at = pl.multiple_of(i * 64, 64)
        for total in sums:
            total[pl.ds(at, 64), :] = jnp.zeros((64, 128), F32)
        return 0

    lax.fori_loop(0, ROWS_OWN // 64, clear, 0)
    tails.wait()
    values = tail_ref.reshape(DEVS, 128)[...].astype(jnp.int32)
    lane = lax.broadcasted_iota(jnp.int32, values.shape, 1)
    over_ref[0, 0] = jnp.max(jnp.where(lane == 127, values, 0))
    late_ref[...] = values
    values = jnp.where((lane >= D) & (lane < D + MAIN), values, ROWS_OWN)
    filled = values < ROWS_OWN
    count = jnp.sum(filled.astype(jnp.int32), axis=1, keepdims=True)
    clash = jnp.zeros(values.shape, jnp.int32)
    for shift in range(2, 16, 2):
        moved = pltpu.roll(values, shift, 1)
        same = filled & (moved == values) & ((lane & 15) >= shift)
        clash = clash | same.astype(jnp.int32)
    clashes = jnp.sum(clash, axis=1, keepdims=True)
    later = pltpu.roll(jnp.where(clash > 0, values, ROWS_OWN), D, 1)
    spots = jnp.where(lane < D, later, jnp.where(clash > 0, ROWS_OWN, values))
    mode = jnp.where(count > 32, 1, 0) + jnp.where(clashes > 0, 2, 0)
    spot_ref[...] = jnp.where(lane == 60, mode, jnp.where(lane == 61, count, spots))
    for k in range(PIECES):
        spots_copy(k).start()

    def batch(s, start, stop):
        parts = []
        for first in range(start, stop, 8):
            rows = range(first, min(first + 8, stop))
            for side in range(2):
                total = sums[2 * (first // 8 % 2) + side]
                at = [land_ref[s, D + 2 * row + side] for row in rows]
                add = [
                    total[pl.ds(spot, 1), :] + new_ref[s, row] for spot, row in zip(at, rows)
                ]
                parts.append((total, at, add))
        for total, at, add in parts:
            for spot, value in zip(at, add):
                total[pl.ds(spot, 1), :] = value

    def sources(i, _):
        for k in range(ADD_STEP):
            batch(i * ADD_STEP + k, 0, 16)
        for k in range(ADD_STEP):
            s = i * ADD_STEP + k
            mode = land_ref[s, 60]

            @pl.when(mode > 0)
            def _():
                @pl.when((mode & 1) == 1)
                def _():
                    batch(s, 16, ROWS)

                @pl.when(mode >= 2)
                def _():
                    def single(j, _):
                        for side in range(2):
                            sums[side][pl.ds(land_ref[s, 2 * j + side], 1), :] += new_ref[s, j]
                        return 0

                    lax.fori_loop(0, (land_ref[s, 61] + 1) >> 1, single, 0)

        return 0

    def piece(k, _):
        spots_copy(k).wait()
        rows_copy(k).wait()
        lax.fori_loop(k * (PIECE // ADD_STEP), (k + 1) * (PIECE // ADD_STEP), sources, 0)
        return 0

    lax.fori_loop(0, PIECES, piece, 0)
    lanes = lax.broadcasted_iota(jnp.int32, (128, 128), 1) < D
    for table in range(TAB_OWN):
        for block in range(ROWS_DEV // 128):
            at = table * ROWS_DEV + block * 128
            at = slice(at, at + 128)
            joined = jnp.where(
                lanes, sums[0][at, :] + sums[2][at, :], sums[1][at, :] + sums[3][at, :]
            )
            turned = joined.T
            turn_ref[table, :, block * 128 : (block + 1) * 128] = turned[:D] + turned[D:]
        table_copy(table).start()
    for table in range(TAB_OWN):
        table_copy(table).wait()


def late_kernel(spot_ref, rest_ref, in_ref, out_ref):
    out_ref[...] = in_ref[...]
    lane = lax.broadcasted_iota(jnp.int32, (D, 128), 1)

    def source(s, _):
        for j in range(PLACES - MAIN):
            spot = spot_ref[s, j]

            @pl.when(spot < ROWS_OWN)
            def _():
                row = rest_ref[s, j // 2][:, (j % 2) * D : (j % 2 + 1) * D]
                column = jnp.sum(diagonal(row, D), axis=1, keepdims=True)
                at = pl.multiple_of((spot & 1023) >> 7 << 7, 128)
                added = jnp.where(lane == (spot & 127), column, 0.0)
                out_ref[spot >> 10, :, pl.ds(at, 128)] += added

        return 0

    lax.fori_loop(0, DEVS, source, 0)


def params(semantics=None):
    return pltpu.CompilerParams(vmem_limit_bytes=VMEM_BYTES, dimension_semantics=semantics)


def send_side(
    event_embed, target, pooled_grad, event_table, event_row, table_slot, lengths, caps,
    w_first, b_first, w_second, b_second, w_score,
):
    smem = pl.BlockSpec(memory_space=pltpu.SMEM)
    whole = lambda *shape: pl.BlockSpec(shape, lambda i: (0,) * len(shape))
    return pl.pallas_call(
        send_kernel,
        grid=(STEPS,),
        in_specs=[
            smem,
            smem,
            pl.BlockSpec((SPAN, LMAX), lambda i: (i, 0)),
            pl.BlockSpec((SPAN, LMAX), lambda i: (i, 0)),
            whole(1, LMAX),
            pl.BlockSpec((B_DEV, STEP, D, LMAX), lambda i: (0, i, 0, 0)),
            pl.BlockSpec((STEP, B_DEV, D), lambda i: (i, 0, 0)),
            pl.BlockSpec((STEP, B_DEV, D), lambda i: (i, 0, 0)),
            pl.BlockSpec((STEP, H1, 4 * D), lambda i: (i, 0, 0)),
            whole(F, H1),
            pl.BlockSpec((STEP, H2, H1), lambda i: (i, 0, 0)),
            whole(F, H2),
            whole(F, H2),
        ],
        out_specs=[pl.BlockSpec(memory_space=pl.ANY)] * 2,
        out_shape=[
            jax.ShapeDtypeStruct((DEVS, ROWS, 1, 128), F32),
            jax.ShapeDtypeStruct((DEVS, LATE, 1, 128), F32),
        ],
        scratch_shapes=[
            pltpu.VMEM((BLOCK, BLOCK + LMAX), BF),
            pltpu.VMEM((DEVS, LMAX), F32),
            pltpu.VMEM((DEVS, LMAX), F32),
            pltpu.VMEM((SPAN, LMAX), jnp.int32),
            pltpu.SMEM((SPAN, LMAX), jnp.int32),
            pltpu.VMEM((DUMMY + 8, 128), F32),
            pltpu.VMEM((EVENTS, 128), F32),
            pltpu.VMEM((DEVS, ROWS, 1, 128), F32),
            pltpu.VMEM((DEVS, LATE, 1, 128), F32),
            pltpu.SemaphoreType.DMA,
            pltpu.SemaphoreType.DMA((2, DEVS // CHUNK)),
        ],
        compiler_params=params(("arbitrary",)),
    )(
        lengths,
        caps,
        event_table.transpose(1, 0, 2).reshape(PAIRS, LMAX),
        event_row.transpose(1, 0, 2).reshape(PAIRS, LMAX),
        table_slot.reshape(1, -1),
        event_embed.transpose(0, 1, 3, 2),
        target.transpose(1, 0, 2),
        pooled_grad.transpose(1, 0, 2),
        w_first.transpose(0, 2, 1),
        b_first,
        w_second.transpose(0, 2, 1),
        b_second,
        w_score,
    )


def receive_side(arrived, late, exchange):
    summed, over, places = pl.pallas_call(
        add_kernel,
        in_specs=[pl.BlockSpec(memory_space=pl.ANY)],
        out_specs=[
            pl.BlockSpec(memory_space=pl.ANY),
            pl.BlockSpec(memory_space=pltpu.SMEM),
            pl.BlockSpec(memory_space=pltpu.VMEM),
        ],
        out_shape=[
            jax.ShapeDtypeStruct((TAB_OWN, D, ROWS_DEV), F32),
            jax.ShapeDtypeStruct((1, 1), jnp.int32),
            jax.ShapeDtypeStruct((DEVS, 128), jnp.int32),
        ],
        scratch_shapes=[
            pltpu.VMEM((DEVS, ROWS, 1, 128), F32),
            pltpu.VMEM((DEVS, 1, 128), F32),
            pltpu.VMEM((DEVS, 128), jnp.int32),
            pltpu.SMEM((DEVS, 128), jnp.int32),
            pltpu.VMEM((TAB_OWN, D, ROWS_DEV), F32),
            pltpu.SemaphoreType.DMA((1 + 2 * PIECES + TAB_OWN,)),
        ]
        + [pltpu.VMEM((ROWS_OWN + 8, 128), F32)] * 4,
        compiler_params=params(),
    )(arrived)

    def add_late(state):
        over, total = state
        spots = places[:, D + MAIN : D + PLACES]
        total = pl.pallas_call(
            late_kernel,
            in_specs=[pl.BlockSpec(memory_space=pltpu.SMEM)]
            + [pl.BlockSpec(memory_space=pltpu.VMEM)] * 2,
            out_specs=pl.BlockSpec(memory_space=pltpu.VMEM),
            out_shape=jax.ShapeDtypeStruct(total.shape, F32),
            compiler_params=params(),
        )(spots, exchange(late), total)
        return jnp.zeros_like(over), total

    _, summed = lax.while_loop(lambda state: state[0][0, 0] > 0, add_late, (over, summed))
    return summed.transpose(0, 2, 1)


def per_device(*args):
    main, late = send_side(*args)
    exchange = functools.partial(
        lax.all_to_all, axis_name=("group", "local"), split_axis=0, concat_axis=0, tiled=True
    )
    return receive_side(exchange(main), late, exchange)


def solution(mesh):
    parted = ("group", "local")
    in_specs = (
        P(parted, None, None, None),
        P(parted, None, None),
        P(parted, None, None),
        P(parted, None, None),
        P(parted, None, None),
        P(),
        P(parted, None),
        P(),
        P(),
        P(),
        P(),
        P(),
        P(),
    )
    return jax.shard_map(
        per_device, mesh=mesh, in_specs=in_specs, out_specs=P("group", "local", None), check_vma=False
    )
```

time: 168 us -> 149 us (0.89)
  blocking collectives: 115 us -> 104 us
  Pallas kernels: 51.7 us -> 44.2 us
    all_to_all x1, blocking collectives: 115 us -> 104 us  [per_device(): return receive_side(exchange(main), late, exchange)]
    pallas_call x3 -> x2, Pallas kernels: 51.7 us -> 44.2 us  [the longest x1 25.7 us: send_side(): pl.pallas_call(send_kernel, grid=(STEPS,), in_specs=[smem, smem, pl.Block...]
where the time goes in v3:
time: 149 us
  blocking collectives  104 us (70%)
  Pallas kernels  44.2 us (30%)
    all_to_all x1, blocking collectives, per_device(): return receive_side(exchange(main), late, exchange)  104 us
    pallas_call x1, Pallas kernels, send_side(): pl.pallas_call(send_kernel, grid=(STEPS,), in_specs=[smem, smem, pl.Block...  25.7 us
    pallas_call x1, Pallas kernels, receive_side(): pl.pallas_call(add_kernel, in_specs=[pl.BlockSpec(memory_space=pl.ANY)],...  18.5 us

profile of v3, /device:TPU:1, one launch (start us, length us, event | category | flops | bytes accessed | tf_op | source)
XLA Modules:
  0.0 149.0 jit_solution(16321701565376885752)
XLA Ops:
  0.0 25.7 %shard_map.127 = (f32[256,28,1,128]{3,2,1,0:T(1,128)}, f32[256,4,1,128]{3,2,1,0:T(1,128)}) custom-call(s32[4,20]{1,0:T(4,128)} %len_ref.1, s32[20]{0:T(128)} %cap_ref.1, s32[80,128]{1,0:T(8,128)} %bitcast.17, s32[80,128]{1,0:T(8,128)} %bitcast.18, s32[1,128]{1,0:T(1,128)} %bitcast.21, bf16[4,20,64,128]{3,2,1,0:T(8,128)(2,1)} %bitcast.15, ...), custom_call_target="tpu_custom_call" | custom-call | tf_op jit(solution)/shard_map/pallas_call | solution.py:436
  25.7 104.2 %all_to_all.9.in_ref = f32[256,28,1,128]{3,2,1,0:T(1,128)} all-to-all(f32[256,28,1,128]{3,2,1,0:T(1,128)} %get-tuple-element.31), channel_id=1, replica_groups=mesh['group'=16,'local'=16] {'group','local'}, dimensions={0} | all-to-all | bytes 7340032 | tf_op jit(solution)/shard_map/all_to_all | solution.py:538
  129.9 18.5 %shard_map.128 = (f32[8,64,1024]{2,1,0:T(8,128)}, s32[1,1]{1,0:T(1,128)}, s32[256,128]{1,0:T(8,128)S(1)}) custom-call(f32[256,28,1,128]{3,2,1,0:T(1,128)} %all_to_all.9.in_ref), custom_call_target="tpu_custom_call" | custom-call | tf_op jit(solution)/shard_map/pallas_call | solution.py:491
  148.5 0.5 while.9

commit v4 on v3

--- a/solution.py
+++ b/solution.py
@@ -16,7 +16,7 @@
 B_DEV = 4
 TAB_OWN = 8
 ROWS_DEV = 1024
-LOCALS = 16
+GROUPS = 16
 DEVS = 256
 PAIRS = B_DEV * F
 ROWS_OWN = TAB_OWN * ROWS_DEV
@@ -58,12 +58,13 @@
 
 
 def rank_events(step, len_ref, cap_ref, table_ref, row_ref, places_ref, earlier_ref, carry_ref, place_ref, slots_ref):
-    table = table_ref[...]
+    block = pl.ds(pl.multiple_of(step * SPAN, SPAN), SPAN)
+    table = table_ref[block, :]
     place = jnp.take_along_axis(
         jnp.broadcast_to(places_ref[...], table.shape), table, axis=1, mode="promise_in_bounds"
     )
-    row = row_ref[...]
-    devs = (place >> 3) * LOCALS + (row >> 10)
+    row = row_ref[block, :]
+    devs = (row >> 10) * GROUPS + (place >> 3)
     owns = (place & 7) * ROWS_DEV + (row & 1023)
     highs = ((owns >> 7) + 1).astype(F32)
     lows = (owns & 127).astype(F32)
@@ -116,7 +117,7 @@
     folds, ups, pre1, dscore, b2, ws, w2t_all, w2_all = ([] for _ in range(8))
     for k in range(STEP):
         f = step * STEP + k
-        w1 = w1_ref[k]
+        w1 = w1_ref[f]
         wa, wb, wc, wd = (w1[:, i * D : (i + 1) * D] for i in range(4))
         wad = wa + wd
         wbd = wb - wd
@@ -128,16 +129,16 @@
         )
         b2.append(jnp.sum(diagonal(b2_ref[pl.ds(f, 1), :], H2_PAD), axis=1, keepdims=True))
         ws.append(jnp.sum(diagonal(ws_ref[pl.ds(f, 1), :], H2_PAD), axis=1, keepdims=True))
-        w2t = jnp.concatenate([w2_ref[k], jnp.zeros((H2_PAD - H2, H1), F32)], axis=0)
+        w2t = jnp.concatenate([w2_ref[f], jnp.zeros((H2_PAD - H2, H1), F32)], axis=0)
         w2t_hi, w2t_lo = split(w2t)
         w2_hi, w2_lo = split(w2t.T)
         w2t_all.append(jnp.concatenate([w2t_hi, w2t_lo, w2t_hi], axis=1))
         w2_all.append(jnp.concatenate([w2_hi, w2_lo, w2_hi], axis=1))
         firsts = []
         for n in range(B_DEV):
-            events = event_ref[n, k]
-            query = query_ref[k, n : n + 1, :].astype(F32)
-            up = up_ref[k, n : n + 1, :].astype(F32)
+            events = event_ref[n, f]
+            query = query_ref[f, n : n + 1, :].astype(F32)
+            up = up_ref[f, n : n + 1, :].astype(F32)
             query = jnp.concatenate([query, query], axis=1)
             up = jnp.concatenate([up, up], axis=1)
             folded = wad + wcc * query
@@ -206,93 +207,102 @@
     carry_ref,
     place_ref,
     slots_ref,
-    index_ref,
+    index_a_ref,
+    index_b_ref,
     bucket_ref,
-    grad_ref,
+    grad_a_ref,
+    grad_b_ref,
     pack_ref,
     rest_ref,
-    slot_sem,
+    slot_sems,
     sems,
 ):
-    step = pl.program_id(0)
-
-    def slot_copy():
-        return pltpu.make_async_copy(slots_ref, index_ref, slot_sem)
-
-    def scatter():
+    index_refs = (index_a_ref, index_b_ref)
+    grad_refs = (grad_a_ref, grad_b_ref)
+
+    def slot_copy(side):
+        return pltpu.make_async_copy(slots_ref.at[side], index_refs[side], slot_sems.at[side])
+
+    def scatter(side):
         for t in range(EVENTS):
-            slot = index_ref[t // LMAX, t % LMAX]
-            bucket_ref[pl.ds(slot, 1), :] = grad_ref[t : t + 1, :]
-
-    @pl.when(step == 0)
-    def _():
-        rows = lax.broadcasted_iota(jnp.int32, (BLOCK, BLOCK + LMAX), 0)
-        cols = lax.broadcasted_iota(jnp.int32, (BLOCK, BLOCK + LMAX), 1)
-        earlier_ref[...] = jnp.where(rows < cols, 1.0, 0.0).astype(BF)
-        carry_ref[...] = jnp.zeros_like(carry_ref)
-        place_ref[...] = jnp.zeros_like(place_ref)
-        slots_ref[...] = jnp.full(slots_ref.shape, DUMMY, jnp.int32)
-        slot_copy().start()
-        slot_copy().wait()
-
-    scatter()
-    rank_events(
-        step, len_ref, cap_ref, table_ref, row_ref, places_ref, earlier_ref, carry_ref, place_ref,
-        slots_ref,
-    )
-    event_grads(step, event_ref, query_ref, up_ref, w1_ref, b1_ref, w2_ref, b2_ref, ws_ref, grad_ref)
-    slot_copy().start()
-    slot_copy().wait()
-
-    @pl.when(step == STEPS - 1)
-    def _():
-        scatter()
-        parts = place_ref[...]
-        high = pltpu.roll(parts, BUCKET, 1)
-        lane = lax.broadcasted_iota(jnp.int32, parts.shape, 1)
-        over = (jnp.max(carry_ref[...]) > float(MAIN)).astype(F32)
-        spots = jnp.where(high > 0.0, high * 128.0 + parts - 128.0, float(ROWS_OWN))
-        place_ref[...] = jnp.where(lane == 127, over, spots)
-        main = pack_ref.reshape(DEVS * ROWS, 128)
-        rest = rest_ref.reshape(DEVS * LATE, 128)
-        lanes = lax.broadcasted_iota(jnp.int32, (HALF, 128), 1) < D
-
-        def copies(chunk):
-            part = pl.ds(chunk * CHUNK, CHUNK)
-            return (
-                pltpu.make_async_copy(pack_ref.at[part], main_ref.at[part], sems.at[0, chunk]),
-                pltpu.make_async_copy(rest_ref.at[part], late_ref.at[part], sems.at[1, chunk]),
+            slot = index_refs[side][t // LMAX, t % LMAX]
+            bucket_ref[pl.ds(slot, 1), :] = grad_refs[side][t : t + 1, :]
+
+    rows = lax.broadcasted_iota(jnp.int32, (BLOCK, BLOCK + LMAX), 0)
+    cols = lax.broadcasted_iota(jnp.int32, (BLOCK, BLOCK + LMAX), 1)
+    earlier_ref[...] = jnp.where(rows < cols, 1.0, 0.0).astype(BF)
+    carry_ref[...] = jnp.zeros_like(carry_ref)
+    place_ref[...] = jnp.zeros_like(place_ref)
+    slots_ref[...] = jnp.full(slots_ref.shape, DUMMY, jnp.int32)
+    slot_copy(0).start()
+    slot_copy(1).start()
+    slot_copy(0).wait()
+
+    def two_steps(i, _):
+        for side in range(2):
+            step = i * 2 + side
+            scatter(side)
+            rank_events(
+                step, len_ref, cap_ref, table_ref, row_ref, places_ref, earlier_ref, carry_ref,
+                place_ref, slots_ref.at[side],
             )
-
-        def pack(chunk, _):
-            def two(k, _):
-                pair = chunk * (CHUNK // 2) + k
-                blocks = []
-                for side in range(2):
-                    dev = pair * 2 + side
-                    at = pl.multiple_of(dev * BUCKET, BUCKET)
-                    bucket_ref[pl.ds(at + HALF + ROWS - 1, 1), :] = place_ref[pl.ds(dev, 1), :]
-                    left = bucket_ref[pl.ds(at, HALF), :]
-                    right = bucket_ref[pl.ds(pl.multiple_of(at + HALF, HALF), HALF), :]
-                    blocks.append(jnp.where(lanes, left, right))
-                at = pl.multiple_of(pair * (2 * ROWS), 2 * ROWS)
-                main[pl.ds(at, 2 * ROWS), :] = jnp.concatenate([b[:ROWS] for b in blocks], axis=0)
-                at = pl.multiple_of(pair * (2 * LATE), 2 * LATE)
-                rest[pl.ds(at, 2 * LATE), :] = jnp.concatenate([b[ROWS:] for b in blocks], axis=0)
-                return 0
-
-            lax.fori_loop(0, CHUNK // 2, two, 0, unroll=4)
-            for copy in copies(chunk):
-                copy.start()
+            event_grads(
+                step, event_ref, query_ref, up_ref, w1_ref, b1_ref, w2_ref, b2_ref, ws_ref,
+                grad_refs[side],
+            )
+            slot_copy(1 - side).wait()
+            slot_copy(side).start()
+        return 0
+
+    lax.fori_loop(0, STEPS // 2, two_steps, 0)
+    scatter(0)
+    slot_copy(1).wait()
+    scatter(1)
+    parts = place_ref[...]
+    high = pltpu.roll(parts, BUCKET, 1)
+    lane = lax.broadcasted_iota(jnp.int32, parts.shape, 1)
+    over = (jnp.max(carry_ref[...]) > float(MAIN)).astype(F32)
+    spots = jnp.where(high > 0.0, high * 128.0 + parts - 128.0, float(ROWS_OWN))
+    place_ref[...] = jnp.where(lane == 127, over, spots)
+    lanes = lax.broadcasted_iota(jnp.int32, (HALF, 128), 1) < D
+
+    def copies(chunk):
+        part = pl.ds(chunk * (CHUNK * ROWS), CHUNK * ROWS)
+        late = pl.ds(chunk * (CHUNK * LATE), CHUNK * LATE)
+        return (
+            pltpu.make_async_copy(pack_ref.at[part], main_ref.at[part], sems.at[0, chunk]),
+            pltpu.make_async_copy(rest_ref.at[late], late_ref.at[late], sems.at[1, chunk]),
+        )
+
+    def pack(chunk, _):
+        def two(k, _):
+            pair = chunk * (CHUNK // 2) + k
+            blocks = []
+            for side in range(2):
+                dev = pair * 2 + side
+                at = pl.multiple_of(dev * BUCKET, BUCKET)
+                bucket_ref[pl.ds(at + HALF + ROWS - 1, 1), :] = place_ref[pl.ds(dev, 1), :]
+                left = bucket_ref[pl.ds(at, HALF), :]
+                right = bucket_ref[pl.ds(pl.multiple_of(at + HALF, HALF), HALF), :]
+                blocks.append(jnp.where(lanes, left, right))
+            at = pl.multiple_of(pair * (2 * ROWS), 2 * ROWS)
+            pack_ref[pl.ds(at, 2 * ROWS), :] = jnp.concatenate([b[:ROWS] for b in blocks], axis=0)
+            at = pl.multiple_of(pair * (2 * LATE), 2 * LATE)
+            rest_ref[pl.ds(at, 2 * LATE), :] = jnp.concatenate([b[ROWS:] for b in blocks], axis=0)
             return 0
 
-        def finish(chunk, _):
-            for copy in copies(chunk):
-                copy.wait()
-            return 0
-
-        lax.fori_loop(0, DEVS // CHUNK, pack, 0)
-        lax.fori_loop(0, DEVS // CHUNK, finish, 0)
+        lax.fori_loop(0, CHUNK // 2, two, 0, unroll=4)
+        for copy in copies(chunk):
+            copy.start()
+        return 0
+
+    def finish(chunk, _):
+        for copy in copies(chunk):
+            copy.wait()
+        return 0
+
+    lax.fori_loop(0, DEVS // CHUNK, pack, 0)
+    lax.fori_loop(0, DEVS // CHUNK, finish, 0)
 
 
 def add_kernel(in_ref, out_ref, over_ref, late_ref, new_ref, tail_ref, spot_ref, land_ref, turn_ref, sems, *sums):
@@ -313,13 +323,16 @@
     for k in range(PIECES):
         rows_copy(k).start()
 
-    def clear(i, _):
-        at = pl.multiple_of(i * 64, 64)
-        for total in sums:
-            total[pl.ds(at, 64), :] = jnp.zeros((64, 128), F32)
-        return 0
-
-    lax.fori_loop(0, ROWS_OWN // 64, clear, 0)
+    def clear(totals):
+        def rows(i, _):
+            at = pl.multiple_of(i * 64, 64)
+            for total in totals:
+                total[pl.ds(at, 64), :] = jnp.zeros((64, 128), F32)
+            return 0
+
+        lax.fori_loop(0, ROWS_OWN // 64, rows, 0)
+
+    clear(sums[:2])
     tails.wait()
     values = tail_ref.reshape(DEVS, 128)[...].astype(jnp.int32)
     lane = lax.broadcasted_iota(jnp.int32, values.shape, 1)
@@ -336,15 +349,17 @@
     clashes = jnp.sum(clash, axis=1, keepdims=True)
     later = pltpu.roll(jnp.where(clash > 0, values, ROWS_OWN), D, 1)
     spots = jnp.where(lane < D, later, jnp.where(clash > 0, ROWS_OWN, values))
-    mode = jnp.where(count > 32, 1, 0) + jnp.where(clashes > 0, 2, 0)
+    mode = jnp.where(count > 32, 1, 0) + jnp.where(count > 40, 1, 0)
+    mode = mode + jnp.where(clashes > 0, 4, 0)
     spot_ref[...] = jnp.where(lane == 60, mode, jnp.where(lane == 61, count, spots))
     for k in range(PIECES):
         spots_copy(k).start()
+    clear(sums[2:])
 
     def batch(s, start, stop):
         parts = []
-        for first in range(start, stop, 8):
-            rows = range(first, min(first + 8, stop))
+        for first in [start] + [row for row in range(start + 1, stop) if row % 8 == 0]:
+            rows = range(first, min(first // 8 * 8 + 8, stop))
             for side in range(2):
                 total = sums[2 * (first // 8 % 2) + side]
                 at = [land_ref[s, D + 2 * row + side] for row in rows]
@@ -365,11 +380,15 @@
 
             @pl.when(mode > 0)
             def _():
-                @pl.when((mode & 1) == 1)
+                @pl.when((mode & 3) > 0)
                 def _():
-                    batch(s, 16, ROWS)
-
-                @pl.when(mode >= 2)
+                    batch(s, 16, 20)
+
+                @pl.when((mode & 3) > 1)
+                def _():
+                    batch(s, 20, ROWS)
+
+                @pl.when(mode >= 4)
                 def _():
                     def single(j, _):
                         for side in range(2):
@@ -423,8 +442,8 @@
     lax.fori_loop(0, DEVS, source, 0)
 
 
-def params(semantics=None):
-    return pltpu.CompilerParams(vmem_limit_bytes=VMEM_BYTES, dimension_semantics=semantics)
+def params():
+    return pltpu.CompilerParams(vmem_limit_bytes=VMEM_BYTES)
 
 
 def send_side(
@@ -432,44 +451,31 @@
     w_first, b_first, w_second, b_second, w_score,
 ):
     smem = pl.BlockSpec(memory_space=pltpu.SMEM)
-    whole = lambda *shape: pl.BlockSpec(shape, lambda i: (0,) * len(shape))
+    vmem = pl.BlockSpec(memory_space=pltpu.VMEM)
     return pl.pallas_call(
         send_kernel,
-        grid=(STEPS,),
-        in_specs=[
-            smem,
-            smem,
-            pl.BlockSpec((SPAN, LMAX), lambda i: (i, 0)),
-            pl.BlockSpec((SPAN, LMAX), lambda i: (i, 0)),
-            whole(1, LMAX),
-            pl.BlockSpec((B_DEV, STEP, D, LMAX), lambda i: (0, i, 0, 0)),
-            pl.BlockSpec((STEP, B_DEV, D), lambda i: (i, 0, 0)),
-            pl.BlockSpec((STEP, B_DEV, D), lambda i: (i, 0, 0)),
-            pl.BlockSpec((STEP, H1, 4 * D), lambda i: (i, 0, 0)),
-            whole(F, H1),
-            pl.BlockSpec((STEP, H2, H1), lambda i: (i, 0, 0)),
-            whole(F, H2),
-            whole(F, H2),
-        ],
+        in_specs=[smem] * 2 + [vmem] * 11,
         out_specs=[pl.BlockSpec(memory_space=pl.ANY)] * 2,
         out_shape=[
-            jax.ShapeDtypeStruct((DEVS, ROWS, 1, 128), F32),
-            jax.ShapeDtypeStruct((DEVS, LATE, 1, 128), F32),
+            jax.ShapeDtypeStruct((DEVS * ROWS, 128), F32),
+            jax.ShapeDtypeStruct((DEVS * LATE, 128), F32),
         ],
         scratch_shapes=[
             pltpu.VMEM((BLOCK, BLOCK + LMAX), BF),
             pltpu.VMEM((DEVS, LMAX), F32),
             pltpu.VMEM((DEVS, LMAX), F32),
-            pltpu.VMEM((SPAN, LMAX), jnp.int32),
+            pltpu.VMEM((2, SPAN, LMAX), jnp.int32),
+            pltpu.SMEM((SPAN, LMAX), jnp.int32),
             pltpu.SMEM((SPAN, LMAX), jnp.int32),
             pltpu.VMEM((DUMMY + 8, 128), F32),
             pltpu.VMEM((EVENTS, 128), F32),
-            pltpu.VMEM((DEVS, ROWS, 1, 128), F32),
-            pltpu.VMEM((DEVS, LATE, 1, 128), F32),
-            pltpu.SemaphoreType.DMA,
+            pltpu.VMEM((EVENTS, 128), F32),
+            pltpu.VMEM((DEVS * ROWS, 128), F32),
+            pltpu.VMEM((DEVS * LATE, 128), F32),
+            pltpu.SemaphoreType.DMA((2,)),
             pltpu.SemaphoreType.DMA((2, DEVS // CHUNK)),
         ],
-        compiler_params=params(("arbitrary",)),
+        compiler_params=params(),
     )(
         lengths,
         caps,
@@ -532,8 +538,10 @@
 
 def per_device(*args):
     main, late = send_side(*args)
+    main = main.reshape(DEVS, ROWS, 1, 128)
+    late = late.reshape(DEVS, LATE, 1, 128)
     exchange = functools.partial(
-        lax.all_to_all, axis_name=("group", "local"), split_axis=0, concat_axis=0, tiled=True
+        lax.all_to_all, axis_name=("local", "group"), split_axis=0, concat_axis=0, tiled=True
     )
     return receive_side(exchange(main), late, exchange)
 

time: 149 us -> 143 us (0.960)
  Pallas kernels: 44.2 us -> 41.1 us
  blocking collectives: 104 us -> 101 us
    all_to_all x1, blocking collectives: 104 us -> 101 us  [per_device(): return receive_side(exchange(main), late, exchange)]
    pallas_call x1, Pallas kernels: 25.7 us -> 23.9 us  [send_side(): pl.pallas_call(send_kernel, in_specs=[smem] * 2 + [vmem] * 11, out_specs=...]
where the time goes in v4:
time: 143 us
  blocking collectives  101 us (71%)
  Pallas kernels  41.1 us (29%)
    all_to_all x1, blocking collectives, per_device(): return receive_side(exchange(main), late, exchange)  101 us
    pallas_call x1, Pallas kernels, send_side(): pl.pallas_call(send_kernel, in_specs=[smem] * 2 + [vmem] * 11, out_specs=...  23.9 us
    pallas_call x1, Pallas kernels, receive_side(): pl.pallas_call(add_kernel, in_specs=[pl.BlockSpec(memory_space=pl.ANY)],...  17.2 us

profile of v4, /device:TPU:1, one launch (start us, length us, event | category | flops | bytes accessed | tf_op | source)
XLA Modules:
  0.0 142.9 jit_solution(13442528056032499098)
XLA Ops:
  0.0 23.9 %shard_map.127 = (f32[7168,128]{1,0:T(8,128)}, f32[1024,128]{1,0:T(8,128)}) custom-call(s32[4,20]{1,0:T(4,128)} %len_ref.1, s32[20]{0:T(128)} %cap_ref.1, s32[80,128]{1,0:T(8,128)} %bitcast.22, s32[80,128]{1,0:T(8,128)} %bitcast.23, s32[1,128]{1,0:T(1,128)} %bitcast.26, bf16[4,20,64,128]{3,2,1,0:T(8,128)(2,1)} %bitcast.20, bf16[20,4,64]{2,1,0:T(4,128)(2,1)} %bitcast.24, ...), custom_call_target="tpu_custom_call" | custom-call | tf_op jit(solution)/shard_map/pallas_call | solution.py:455
  23.9 101.2 %all_to_all.9.in_ref = f32[256,28,1,128]{3,2,1,0:T(1,128)} all-to-all(f32[256,28,1,128]{3,2,1,0:T(1,128)} %bitcast.18), channel_id=1, replica_groups=mesh['group'=16,'local'=16] {'local','group'}, dimensions={0} | all-to-all | bytes 7340032 | tf_op jit(solution)/shard_map/all_to_all | solution.py:546
  125.1 17.2 %shard_map.128 = (f32[8,64,1024]{2,1,0:T(8,128)}, s32[1,1]{1,0:T(1,128)}, s32[256,128]{1,0:T(8,128)S(1)}) custom-call(f32[256,28,1,128]{3,2,1,0:T(1,128)} %all_to_all.9.in_ref), custom_call_target="tpu_custom_call" | custom-call | tf_op jit(solution)/shard_map/pallas_call | solution.py:497
  142.4 0.5 while.9

commit v5 on v4

--- a/solution.py
+++ b/solution.py
@@ -33,7 +33,7 @@
 PLACES = 60
 DUMMY = DEVS * BUCKET
 CHUNK = 32
-PIECES = 4
+PIECES = 8
 PIECE = DEVS // PIECES
 ADD_STEP = 4
 BF = jnp.bfloat16
@@ -180,11 +180,15 @@
             ).astype(BF)
             fold_hi, fold_lo = folds[k * B_DEV + n]
             row = (k * B_DEV + n) * LMAX
-            grad_ref[row : row + LMAX, :] = dot(
-                jnp.concatenate([d1_hi[:, at], d1_lo[:, at], d1_hi[:, at], score_rows], axis=0),
-                jnp.concatenate([fold_hi, fold_hi, fold_lo, ups[k * B_DEV + n]], axis=0),
+            parts = dot(
+                d1_hi[:, at], jnp.concatenate([fold_hi, fold_lo], axis=1), ((0,), (0,))
+            )
+            rest = dot(
+                jnp.concatenate([d1_lo[:, at], score_rows], axis=0),
+                jnp.concatenate([fold_hi, ups[k * B_DEV + n]], axis=0),
                 ((0,), (0,)),
             )
+            grad_ref[row : row + LMAX, :] = parts[:, :128] + parts[:, 128:] + rest
 
 
 def send_kernel(

time: 143 us -> 141 us (0.986)
  Pallas kernels: 41.1 us -> 39.6 us
    pallas_call x1, Pallas kernels: 23.9 us -> 22.3 us  [send_side(): pl.pallas_call(send_kernel, in_specs=[smem] * 2 + [vmem] * 11, out_specs=...]
where the time goes in v5:
time: 141 us
  blocking collectives  101 us (72%)
  Pallas kernels  39.6 us (28%)
    all_to_all x1, blocking collectives, per_device(): return receive_side(exchange(main), late, exchange)  101 us
    pallas_call x1, Pallas kernels, send_side(): pl.pallas_call(send_kernel, in_specs=[smem] * 2 + [vmem] * 11, out_specs=...  22.3 us
    pallas_call x1, Pallas kernels, receive_side(): pl.pallas_call(add_kernel, in_specs=[pl.BlockSpec(memory_space=pl.ANY)],...  17.3 us

profile of v5, /device:TPU:1, one launch (start us, length us, event | category | flops | bytes accessed | tf_op | source)
XLA Modules:
  0.0 141.4 jit_solution(1990759066706520576)
XLA Ops:
  0.0 22.3 %shard_map.127 = (f32[7168,128]{1,0:T(8,128)}, f32[1024,128]{1,0:T(8,128)}) custom-call(s32[4,20]{1,0:T(4,128)} %len_ref.1, s32[20]{0:T(128)} %cap_ref.1, s32[80,128]{1,0:T(8,128)} %bitcast.22, s32[80,128]{1,0:T(8,128)} %bitcast.23, s32[1,128]{1,0:T(1,128)} %bitcast.26, bf16[4,20,64,128]{3,2,1,0:T(8,128)(2,1)} %bitcast.20, bf16[20,4,64]{2,1,0:T(4,128)(2,1)} %bitcast.24, ...), custom_call_target="tpu_custom_call" | custom-call | tf_op jit(solution)/shard_map/pallas_call | solution.py:459
  22.3 101.2 %all_to_all.9.in_ref = f32[256,28,1,128]{3,2,1,0:T(1,128)} all-to-all(f32[256,28,1,128]{3,2,1,0:T(1,128)} %bitcast.18), channel_id=1, replica_groups=mesh['group'=16,'local'=16] {'local','group'}, dimensions={0} | all-to-all | bytes 7340032 | tf_op jit(solution)/shard_map/all_to_all | solution.py:550
  123.5 17.3 %shard_map.128 = (f32[8,64,1024]{2,1,0:T(8,128)}, s32[1,1]{1,0:T(1,128)}, s32[256,128]{1,0:T(8,128)S(1)}) custom-call(f32[256,28,1,128]{3,2,1,0:T(1,128)} %all_to_all.9.in_ref), custom_call_target="tpu_custom_call" | custom-call | tf_op jit(solution)/shard_map/pallas_call | solution.py:501
  140.8 0.5 while.9

commit v6 on v5

--- a/solution.py
+++ b/solution.py
@@ -115,6 +115,13 @@
     row_at = lax.broadcasted_iota(jnp.int32, (16, 128), 0)
     lane_at = lax.broadcasted_iota(jnp.int32, (16, 128), 1)
     folds, ups, pre1, dscore, b2, ws, w2t_all, w2_all = ([] for _ in range(8))
+    w2s = jnp.concatenate(
+        [
+            jnp.concatenate([w2_ref[step * STEP + k], jnp.zeros((64 - H2, H1), F32)], axis=0)
+            for k in range(STEP)
+        ],
+        axis=0,
+    ).T
     for k in range(STEP):
         f = step * STEP + k
         w1 = w1_ref[f]
@@ -131,7 +138,7 @@
         ws.append(jnp.sum(diagonal(ws_ref[pl.ds(f, 1), :], H2_PAD), axis=1, keepdims=True))
         w2t = jnp.concatenate([w2_ref[f], jnp.zeros((H2_PAD - H2, H1), F32)], axis=0)
         w2t_hi, w2t_lo = split(w2t)
-        w2_hi, w2_lo = split(w2t.T)
+        w2_hi, w2_lo = split(w2s[:, k * 64 : k * 64 + H2_PAD])
         w2t_all.append(jnp.concatenate([w2t_hi, w2t_lo, w2t_hi], axis=1))
         w2_all.append(jnp.concatenate([w2_hi, w2_lo, w2_hi], axis=1))
         firsts = []

time: 141 us -> 142 us (level)
  no operation moved by 1% of the time
where the time goes in v6:
time: 142 us; the launch traced here: 141 us
  blocking collectives  101 us (71%)
  Pallas kernels  39.5 us (28%)
    all_to_all x1, blocking collectives, per_device(): return receive_side(exchange(main), late, exchange)  101 us
    pallas_call x1, Pallas kernels, send_side(): pl.pallas_call(send_kernel, in_specs=[smem] * 2 + [vmem] * 11, out_specs=...  22.1 us
    pallas_call x1, Pallas kernels, receive_side(): pl.pallas_call(add_kernel, in_specs=[pl.BlockSpec(memory_space=pl.ANY)],...  17.4 us

profile of v6, /device:TPU:1, one launch (start us, length us, event | category | flops | bytes accessed | tf_op | source)
XLA Modules:
  0.0 141.2 jit_solution(15461423254524876686)
XLA Ops:
  0.0 22.1 %shard_map.127 = (f32[7168,128]{1,0:T(8,128)}, f32[1024,128]{1,0:T(8,128)}) custom-call(s32[4,20]{1,0:T(4,128)} %len_ref.1, s32[20]{0:T(128)} %cap_ref.1, s32[80,128]{1,0:T(8,128)} %bitcast.22, s32[80,128]{1,0:T(8,128)} %bitcast.23, s32[1,128]{1,0:T(1,128)} %bitcast.26, bf16[4,20,64,128]{3,2,1,0:T(8,128)(2,1)} %bitcast.20, bf16[20,4,64]{2,1,0:T(4,128)(2,1)} %bitcast.24, ...), custom_call_target="tpu_custom_call" | custom-call | tf_op jit(solution)/shard_map/pallas_call | solution.py:466
  22.1 101.2 %all_to_all.9.in_ref = f32[256,28,1,128]{3,2,1,0:T(1,128)} all-to-all(f32[256,28,1,128]{3,2,1,0:T(1,128)} %bitcast.18), channel_id=1, replica_groups=mesh['group'=16,'local'=16] {'local','group'}, dimensions={0} | all-to-all | bytes 7340032 | tf_op jit(solution)/shard_map/all_to_all | solution.py:557
  123.3 17.4 %shard_map.128 = (f32[8,64,1024]{2,1,0:T(8,128)}, s32[1,1]{1,0:T(1,128)}, s32[256,128]{1,0:T(8,128)S(1)}) custom-call(f32[256,28,1,128]{3,2,1,0:T(1,128)} %all_to_all.9.in_ref), custom_call_target="tpu_custom_call" | custom-call | tf_op jit(solution)/shard_map/pallas_call | solution.py:508
  140.7 0.5 while.9
